TPU v7x, 128 devices: a whole 4x4x4 slice. The times are simulated.
128 devices in a mesh: rows: 16 (over z_hi, x, core), hash: 8 (over y, z_lo).
Axes of the slice: x: 4, y: 4, z: 4 (z_hi: 2, z_lo: 2; z = z_hi * 2 + z_lo), core: 2. Of those that a mesh axis runs over, the one named last changes fastest.
Arguments:
- tokens: bfloat16 [20480, 768], P('rows'), may hold values from -6 to 6
- item_cuts: int32 [4], replicated, may hold values from 0 to 19968, as said below
- q_codes: int32 [8, 12, 20480], P('hash', None, 'rows'), may hold values from 0 to 255
- k_codes: int32 [8, 12, 20480], P('hash', None, 'rows'), may hold values from 0 to 255
- hyperplanes: float32 [8, 64, 8], P('hash'), may hold values from -1.5 to 1.5
- w_query: bfloat16 [768, 768], replicated, may hold values from -0.21875 to 0.21875
- b_query: float32 [768], replicated, may hold values from -1.5 to 1.5
- w_key: bfloat16 [768, 768], replicated, may hold values from -0.21875 to 0.21875
- b_key: float32 [768], replicated, may hold values from -1.5 to 1.5
- w_value: bfloat16 [768, 768], replicated, may hold values from -0.21875 to 0.21875
- b_value: float32 [768], replicated, may hold values from -1.5 to 1.5
- conv_weight: float32 [12, 65], replicated, may hold values from -0.375 to 0.375
- w_out: bfloat16 [768, 768], replicated, may hold values from -0.4375 to 0.4375
- b_out: float32 [768], replicated, may hold values from -1 to 1
- ln1_gain: float32 [768], replicated, may hold values from 0.5 to 1.5
- ln1_bias: float32 [768], replicated, may hold values from -1 to 1
- w_in: bfloat16 [768, 3072], replicated, may hold values from -0.21875 to 0.21875
- b_in: float32 [3072], replicated, may hold values from -1 to 1
- w_back: bfloat16 [3072, 768], replicated, may hold values from -0.109375 to 0.109375
- b_back: float32 [768], replicated, may hold values from -1 to 1
- ln2_gain: float32 [768], replicated, may hold values from 0.5 to 1.5
- ln2_bias: float32 [768], replicated, may hold values from -1 to 1
- cotangent: float32 [20480, 768], P(('rows', 'hash')), may hold values from -6 to 6
Outputs:
- output: float32 [20480, 768], P(('rows', 'hash'))
- grad_tokens: float32 [20480, 768], P(('rows', 'hash'))
- grad_w_query: float32 [768, 768], replicated
- grad_b_query: float32 [768], replicated
- grad_w_key: float32 [768, 768], replicated
- grad_b_key: float32 [768], replicated
- grad_w_value: float32 [768, 768], replicated
- grad_b_value: float32 [768], replicated
- grad_conv_weight: float32 [12, 65], replicated
- grad_w_out: float32 [768, 768], replicated
- grad_b_out: float32 [768], replicated
- grad_ln1_gain: float32 [768], replicated
- grad_ln1_bias: float32 [768], replicated
- grad_w_in: float32 [768, 3072], replicated
- grad_b_in: float32 [3072], replicated
- grad_w_back: float32 [3072, 768], replicated
- grad_b_back: float32 [768], replicated
- grad_ln2_gain: float32 [768], replicated
- grad_ln2_bias: float32 [768], replicated
Inputs may be any that keep to these rules, and one draw needn't show every extreme that they name: item_cuts[0] is 0 and the entries rise; item i holds the positions from item_cuts[i] up to item_cuts[i + 1] (the last item up to 20480); 3 short items hold 512 to 1024 positions each, the last item exactly 512; one long item holds the remaining positions; one or two short items, drawn from the seed, stand before the long one, the first and the last item being short.
All inputs are finite; a program needn't handle non-finite values.
Results may differ from a plain program's by a relative error of at most 0.02.
Values may be sent and summed in bfloat16 or wider, within the bound.
A program may use at most 320 MiB of HBM per device.

v0:
```python
import jax
import jax.numpy as jnp
from jax import lax
from jax.sharding import PartitionSpec as P

SHORT_LEN = 512


EPS_NORM = 1e-05
EPS_UNIT = 1e-06
HIGHEST = lax.Precision.HIGHEST


def with_halo(array, sides, width):
    for axis, dim in sides:
        peers, length = (lax.axis_size(axis), array.shape[dim])
        up = [(i, (i + 1) % peers) for i in range(peers - 1)]
        down = [(j, i) for i, j in up]
        last = lax.slice_in_dim(array, length - width, length, axis=dim)
        leading = lax.slice_in_dim(array, 0, width, axis=dim)
        before = lax.ppermute(last, axis, up)
        after = lax.ppermute(leading, axis, down)
        array = jnp.concatenate([before, array, after], axis=dim)
    return array


def layer_norm(values, norm_gain, norm_bias):
    row_mean = jnp.mean(values, axis=-1, keepdims=True)
    centred = values - row_mean
    spread = jnp.mean(centred * centred, axis=-1, keepdims=True)
    return centred * lax.rsqrt(spread + EPS_NORM) * norm_gain + norm_bias


def gelu_exact(values):
    return jax.nn.gelu(values, approximate=False)


def contract_rows(left, right):
    return lax.dot_general(
        left, right, (((0,), (0,)), ((), ())), preferred_element_type=jnp.float32
    )


def times_transposed(left, right):
    return lax.dot_general(
        left, right, (((1,), (1,)), ((), ())), preferred_element_type=jnp.float32
    )


def code_signs(code_ints, code_bits):
    shifts = jnp.arange(code_bits, dtype=jnp.int32)
    picked = jnp.bitwise_and(jnp.right_shift(code_ints[..., None], shifts), 1)
    return (2 * picked - 1).astype(jnp.float32)


def head_weight(rows_head, signs_head, planes):
    unit_rows = rows_head * lax.rsqrt(
        jnp.sum(rows_head * rows_head, axis=-1, keepdims=True) + EPS_UNIT
    )
    lifted = jnp.einsum("re,seb->srb", unit_rows, planes, precision=HIGHEST)
    return jnp.exp(jnp.sum(signs_head * lifted, axis=-1))


def one_hot_slots(slots_head, width):
    return (slots_head[..., None] == jnp.arange(width, dtype=jnp.int32)).astype(jnp.float32)


def item_number(positions, item_cuts):
    return jnp.sum((positions[:, None] >= item_cuts[None, :]).astype(jnp.int32), axis=1) - 1


def convolve(extended, taps, item_tags):
    out_rows = extended.shape[0] - taps.shape[1] + 1
    conv_half = (taps.shape[1] - 1) // 2
    head_count = taps.shape[0]
    shaped = extended.reshape(extended.shape[0], head_count, extended.shape[1] // head_count)
    own_tags = item_tags[conv_half : conv_half + out_rows]
    running = jnp.zeros((out_rows, head_count, shaped.shape[2]), jnp.float32)
    for tap_index in range(taps.shape[1]):
        same_item = (item_tags[tap_index : tap_index + out_rows] == own_tags).astype(jnp.float32)
        running = (
            running
            + taps[:, tap_index][None, :, None]
            * same_item[:, None, None]
            * shaped[tap_index : tap_index + out_rows]
        )
    return running.reshape(out_rows, extended.shape[1])


def per_device(
    tokens,
    item_cuts,
    q_codes,
    k_codes,
    hyperplanes,
    w_query,
    b_query,
    w_key,
    b_key,
    w_value,
    b_value,
    conv_weight,
    w_out,
    b_out,
    ln1_gain,
    ln1_bias,
    w_in,
    b_in,
    w_back,
    b_back,
    ln2_gain,
    ln2_bias,
    cotangent,
):
    group_rows = tokens.shape[0]
    model_width = tokens.shape[1]
    head_count = conv_weight.shape[0]
    head_dim = model_width // head_count
    conv_half = (conv_weight.shape[1] - 1) // 2
    slice_rows = group_rows // lax.axis_size("hash")
    slice_start = lax.axis_index("hash") * slice_rows
    group_start = lax.axis_index("rows") * group_rows
    stream_len = group_rows * lax.axis_size("rows")
    code_bits = hyperplanes.shape[2]
    per_item = 2**code_bits
    item_count = item_cuts.shape[0]
    window_items = min(item_count, (group_rows - 2) // SHORT_LEN + 2)
    window_slots = window_items * per_item
    own_tokens = lax.dynamic_slice_in_dim(tokens, slice_start, slice_rows, 0)
    query_part = jnp.dot(tokens, w_query, preferred_element_type=jnp.float32) + b_query
    key_part = jnp.dot(tokens, w_key, preferred_element_type=jnp.float32) + b_key
    value_part = jnp.dot(tokens, w_value, preferred_element_type=jnp.float32) + b_value
    own_value = lax.dynamic_slice_in_dim(value_part, slice_start, slice_rows, 0)
    positions = group_start + jnp.arange(group_rows, dtype=jnp.int32)
    item_of = item_number(positions, item_cuts)
    window_first = jnp.minimum(item_of[0], item_count - window_items)
    local_base = ((item_of - window_first) * per_item)[None, None, :]
    key_slot = (local_base + k_codes).transpose(1, 0, 2)
    query_slot = (local_base + q_codes).transpose(1, 0, 2)
    key_signs = code_signs(k_codes, code_bits).transpose(1, 0, 2, 3)
    query_signs = code_signs(q_codes, code_bits).transpose(1, 0, 2, 3)

    def by_heads(matrix_rows):
        return matrix_rows.reshape(group_rows, head_count, head_dim).transpose(1, 0, 2)

    def fill_head(pieces):
        key_head, value_head, signs_head, slots_head = pieces
        key_w = head_weight(key_head, signs_head, hyperplanes)
        hot = one_hot_slots(slots_head, window_slots)
        sums_head = jnp.einsum(
            "srk,sre->ske", hot, key_w[..., None] * value_head[None], precision=HIGHEST
        )
        mass_head = jnp.einsum("srk,sr->sk", hot, key_w, precision=HIGHEST)
        return (sums_head, mass_head)

    def fill_tables(key_in, value_in):
        return lax.map(
            jax.checkpoint(fill_head), (by_heads(key_in), by_heads(value_in), key_signs, key_slot)
        )

    def read_head(pieces):
        query_head, signs_head, slots_head, sums_head, mass_head = pieces
        query_w = head_weight(query_head, signs_head, hyperplanes)
        hot = one_hot_slots(slots_head, window_slots)
        picked = jnp.einsum("srk,ske->sre", hot, sums_head, precision=HIGHEST)
        picked_mass = jnp.einsum("srk,sk->sr", hot, mass_head, precision=HIGHEST)
        return (
            jnp.sum(query_w[..., None] * picked, axis=0),
            jnp.sum(query_w * picked_mass, axis=0),
        )

    def read_tables(query_in, sums_window, mass_window):
        numer_heads, denom_heads = lax.map(
            jax.checkpoint(read_head),
            (by_heads(query_in), query_signs, query_slot, sums_window, mass_window),
        )
        return (numer_heads.transpose(1, 0, 2).reshape(group_rows, model_width), denom_heads.T)

    def place(window_sums, window_mass):
        return (window_sums, window_mass)

    def window_of(whole_sums, whole_mass):
        return (whole_sums, whole_mass)

    (part_sums, part_mass), fill_back = jax.vjp(fill_tables, key_part, value_part)
    placed_sums, placed_mass = place(part_sums, part_mass)
    share_sums, share_mass = (
        lax.psum_scatter(placed_sums, "rows", scatter_dimension=2, tiled=True),
        lax.psum_scatter(placed_mass, "rows", scatter_dimension=2, tiled=True),
    )
    whole_sums, whole_mass = (
        lax.all_gather(share_sums, "rows", axis=2, tiled=True),
        lax.all_gather(share_mass, "rows", axis=2, tiled=True),
    )
    full_sums, full_mass = window_of(whole_sums, whole_mass)
    (part_numer, part_denom), read_back = jax.vjp(read_tables, query_part, full_sums, full_mass)
    numerator, denominator = (
        lax.psum_scatter(part_numer, "hash", scatter_dimension=0, tiled=True),
        lax.psum_scatter(part_denom, "hash", scatter_dimension=0, tiled=True),
    )
    scale_rows = 1.0 / (denominator + 1.0)
    estimate = numerator.reshape(slice_rows, head_count, head_dim) * scale_rows[:, :, None]
    ext_positions = (
        group_start
        + slice_start
        - conv_half
        + jnp.arange(slice_rows + 2 * conv_half, dtype=jnp.int32)
    )
    inside = (ext_positions >= 0) & (ext_positions < stream_len)
    item_tags = jnp.where(inside, item_number(ext_positions, item_cuts) + 1, 0)
    value_ext = with_halo(own_value, ((("rows", "hash"), 0),), conv_half)

    def conv_of_taps(taps):
        return convolve(value_ext, taps, item_tags)

    conv_mix, conv_back = jax.vjp(conv_of_taps, conv_weight)
    attended = estimate.reshape(slice_rows, model_width) + conv_mix
    attended_low = attended.astype(jnp.bfloat16)
    branch = jnp.dot(attended_low, w_out, preferred_element_type=jnp.float32) + b_out
    own_input = own_tokens.astype(jnp.float32)
    hidden, norm_one_back = jax.vjp(layer_norm, own_input + branch, ln1_gain, ln1_bias)
    hidden_low = hidden.astype(jnp.bfloat16)
    inner_pre = jnp.dot(hidden_low, w_in, preferred_element_type=jnp.float32) + b_in
    activated, gelu_back = jax.vjp(gelu_exact, inner_pre)
    activated_low = activated.astype(jnp.bfloat16)
    outer_out = jnp.dot(activated_low, w_back, preferred_element_type=jnp.float32) + b_back
    output, norm_two_back = jax.vjp(layer_norm, hidden + outer_out, ln2_gain, ln2_bias)
    sum_grad, grad_ln2_gain, grad_ln2_bias = norm_two_back(cotangent)
    outer_grad = sum_grad.astype(jnp.bfloat16)
    grad_w_back = contract_rows(activated_low, outer_grad)
    grad_b_back = jnp.sum(outer_grad.astype(jnp.float32), axis=0)
    (inner_grad,) = gelu_back(times_transposed(outer_grad, w_back))
    inner_low = inner_grad.astype(jnp.bfloat16)
    grad_w_in = contract_rows(hidden_low, inner_low)
    grad_b_in = jnp.sum(inner_low.astype(jnp.float32), axis=0)
    hidden_grad = sum_grad + times_transposed(inner_low, w_in)
    resid_grad, grad_ln1_gain, grad_ln1_bias = norm_one_back(hidden_grad)
    branch_grad = resid_grad.astype(jnp.bfloat16)
    grad_w_out = contract_rows(attended_low, branch_grad)
    grad_b_out = jnp.sum(branch_grad.astype(jnp.float32), axis=0)
    attended_grad = times_transposed(branch_grad, w_out).astype(jnp.bfloat16)
    attended_full = attended_grad.astype(jnp.float32)
    grad_heads = attended_full.reshape(slice_rows, head_count, head_dim)
    numer_grad = grad_heads * scale_rows[:, :, None]
    denom_grad = -jnp.sum(numer_grad * estimate, axis=-1)
    numer_all, denom_all = (
        lax.all_gather(numer_grad.reshape(slice_rows, model_width), "hash", axis=0, tiled=True),
        lax.all_gather(denom_grad, "hash", axis=0, tiled=True),
    )
    query_grad, sums_grad, mass_grad = read_back((numer_all, denom_all))
    placed_sums_grad, placed_mass_grad = place(sums_grad, mass_grad)
    share_sums_grad, share_mass_grad = (
        lax.psum_scatter(placed_sums_grad, "rows", scatter_dimension=2, tiled=True),
        lax.psum_scatter(placed_mass_grad, "rows", scatter_dimension=2, tiled=True),
    )
    whole_sums_grad, whole_mass_grad = (
        lax.all_gather(share_sums_grad, "rows", axis=2, tiled=True),
        lax.all_gather(share_mass_grad, "rows", axis=2, tiled=True),
    )
    sums_total, mass_total = window_of(whole_sums_grad, whole_mass_grad)
    key_grad, value_grad = fill_back((sums_total, mass_total))
    query_own, key_own, value_own = (
        lax.psum_scatter(
            query_grad.astype(jnp.bfloat16), "hash", scatter_dimension=0, tiled=True
        ).astype(jnp.float32),
        lax.psum_scatter(
            key_grad.astype(jnp.bfloat16), "hash", scatter_dimension=0, tiled=True
        ).astype(jnp.float32),
        lax.psum_scatter(
            value_grad.astype(jnp.bfloat16), "hash", scatter_dimension=0, tiled=True
        ).astype(jnp.float32),
    )
    grad_ext = with_halo(attended_grad, ((("rows", "hash"), 0),), conv_half)
    value_own = value_own + convolve(grad_ext.astype(jnp.float32), conv_weight[:, ::-1], item_tags)
    (grad_conv_weight,) = conv_back(attended_full)
    query_low = query_own.astype(jnp.bfloat16)
    key_low = key_own.astype(jnp.bfloat16)
    value_low = value_own.astype(jnp.bfloat16)
    grad_w_query = contract_rows(own_tokens, query_low)
    grad_b_query = jnp.sum(query_low.astype(jnp.float32), axis=0)
    grad_w_key = contract_rows(own_tokens, key_low)
    grad_b_key = jnp.sum(key_low.astype(jnp.float32), axis=0)
    grad_w_value = contract_rows(own_tokens, value_low)
    grad_b_value = jnp.sum(value_low.astype(jnp.float32), axis=0)
    grad_tokens = (
        resid_grad
        + times_transposed(query_low, w_query)
        + times_transposed(key_low, w_key)
        + times_transposed(value_low, w_value)
    )
    (
        grad_w_query,
        grad_b_query,
        grad_w_key,
        grad_b_key,
        grad_w_value,
        grad_b_value,
        grad_conv_weight,
        grad_w_out,
        grad_b_out,
        grad_ln1_gain,
        grad_ln1_bias,
        grad_w_in,
        grad_b_in,
        grad_w_back,
        grad_b_back,
        grad_ln2_gain,
        grad_ln2_bias,
    ) = lax.psum(
        (
            grad_w_query,
            grad_b_query,
            grad_w_key,
            grad_b_key,
            grad_w_value,
            grad_b_value,
            grad_conv_weight,
            grad_w_out,
            grad_b_out,
            grad_ln1_gain,
            grad_ln1_bias,
            grad_w_in,
            grad_b_in,
            grad_w_back,
            grad_b_back,
            grad_ln2_gain,
            grad_ln2_bias,
        ),
        ("rows", "hash"),
    )
    return (
        output,
        grad_tokens,
        grad_w_query,
        grad_b_query,
        grad_w_key,
        grad_b_key,
        grad_w_value,
        grad_b_value,
        grad_conv_weight,
        grad_w_out,
        grad_b_out,
        grad_ln1_gain,
        grad_ln1_bias,
        grad_w_in,
        grad_b_in,
        grad_w_back,
        grad_b_back,
        grad_ln2_gain,
        grad_ln2_bias,
    )


def solution(mesh):
    placed = (
        P("rows", None),
        P(),
        P("hash", None, "rows"),
        P("hash", None, "rows"),
        P("hash", None, None),
        P(),
        P(),
        P(),
        P(),
        P(),
        P(),
        P(),
        P(),
        P(),
        P(),
        P(),
        P(),
        P(),
        P(),
        P(),
        P(),
        P(),
        P(("rows", "hash"), None),
    )
    return jax.shard_map(
        per_device,
        mesh=mesh,
        in_specs=placed,
        out_specs=(
            P(("rows", "hash"), None),
            P(("rows", "hash"), None),
            P(),
            P(),
            P(),
            P(),
            P(),
            P(),
            P(),
            P(),
            P(),
            P(),
            P(),
            P(),
            P(),
            P(),
            P(),
            P(),
            P(),
        ),
        check_vma=False,
    )
```

profile of v0, /device:TPU:1, one launch (start us, length us, event | category | flops | bytes accessed | tf_op | source)
XLA Modules:
  0.0 1992.0 jit_solution(14218406602225401355)
XLA Ops:
  34.5 110.8 %while.68 = (s32[]{:T(128)}, f32[12,1,1024,64]{2,3,1,0:T(8,128)}, f32[12,1,1024]{2,1,0:T(1,128)S(1)}, s32[12,1,1280]{2,1,0:T(1,128)S(1)}, f32[12,1,1280,8]{2,3,1...) while((s32[]{:T(128)}, f32[12,1,1024,64]{2,3,1,0:T(8,128)}, ...), condition=%wide.region_4.5_spmd.clone.clone.clone, body=%wide.region_1.4_spmd.clone.clone.sunk.clone | while | flops 1033194240 | bytes 3012197 | solution.py:157
  145.4 15.3 copy.914
  160.7 57.2 %bitcast_reduce_fusion.2 = f32[1024,12,64]{2,1,0:T(8,128)} fusion(f32[12,1,1024,64]{3,1,0,2:T(1,128)} %copy.914), kind=kLoop, calls=%fused_computation.209 | loop fusion | bytes 6291456
  217.9 7.2 reshape.6432
  242.0 6.9 bitcast_reduce_fusion.1
  265.2 37.5 %reduce-scatter.28.cloned.1.call-done = f32[64,768]{1,0:T(8,128)} async-done(((f32[1024,768]{1,0:T(8,128)}), f32[64,768]{1,0:T(8,128)}) %reduce-scatter.28.cloned.1.call-update) | async-done | bytes 196624
  307.5 62.9 %reduce-scatter.30.cloned.1.call-done = f32[64,12]{1,0:T(8,128)} async-done(((f32[1024,12]{1,0:T(8,128)}), f32[64,12]{1,0:T(8,128)}) %reduce-scatter.30.cloned.1.call-update) | async-done | bytes 3088
  371.9 25.5 %all_gather.19 = f32[12,1,1024]{0,1,2:T(1,128)S(1)} all-gather(f32[12,1,64]{0,1,2:T(1,128)S(1)} %copy.701), channel_id=1, replica_groups=mesh['rows'=16,'hash'=8] {'rows'}, dimensions={2}, use_global_device_ids=true | all-gather | bytes 52224 | tf_op jit(solution)/shard_map/all_gather | solution.py:193
  398.3 41.4 %all-gather.5.cloned.1.call-done = f32[12,1,1024,64]{3,1,0,2:T(1,128)} async-done(((f32[12,1,64,64]{3,1,0,2:T(1,128)}), f32[12,1,1024,64]{3,1,0,2:T(1,128)}) %all-gather.5.cloned.1.call-update) | async-done | bytes 3145744 | tf_op jit(solution)/shard_map/all_gather | solution.py:192
  445.8 129.3 %while.67 = (s32[]{:T(128)}, f32[12,1280,64]{1,2,0:T(8,128)}, f32[12,1280]{1,0:T(8,128)S(1)}, f32[12,1,1280,8]{2,3,1,0:T(8,128)S(1)}, f32[12,1280,64]{2,1,0:T(8,...) while((s32[]{:T(128)}, f32[12,1280,64]{1,2,0:T(8,128)}, ...), condition=%wide.region_10.11_spmd.clone.clone, body=%wide.region_7.10_spmd.clone.sunk.clone | while | flops 1033195520 | bytes 1982057 | solution.py:173
  659.9 39.5 %reduce-scatter.22.cloned.1.call-done = f32[160,768]{1,0:T(8,128)} async-done(((f32[1280,768]{1,0:T(8,128)}), f32[160,768]{1,0:T(8,128)}) %reduce-scatter.22.cloned.1.call-update) | async-done | bytes 491536 | tf_op jit(solution)/shard_map/reduce_scatter | solution.py:198
  699.4 24.2 %add_convert_fusion.1 = (bf16[160,768]{1,0:T(8,128)(2,1)S(1)}, f32[160,768]{1,0:T(8,128)}, f32[160,768]{1,0:T(8,128)}, f32[160,768]{1,0:T(8,128)}, f32[160,768]{...) fusion(f32[160,768]{1,0:T(8,128)} %copy.769, ...), kind=kLoop, calls=%fused_computation.581 | loop fusion | flops 24084480 | bytes 63851520 | tf_op jit(solution)/shard_map/convert_element_type | solution.py:218
  784.7 25.3 %all-gather = f32[8,160,12]{1,2,0:T(8,128)S(1)} all-gather(f32[1,160,12]{1,2,0:T(8,128)S(1)} %negate_bitcast_fusion), channel_id=1, replica_groups=mesh['rows'=16,'hash'=8] {'hash'}, dimensions={0}, use_global_device_ids=true | all-gather | bytes 69120 | tf_op jit(solution)/shard_map/all_gather | solution.py:248
  810.8 28.8 %all-gather.7.cloned.1.call-done = f32[1280,768]{1,0:T(8,128)} async-done(((f32[160,768]{1,0:T(8,128)}), f32[1280,768]{1,0:T(8,128)}) %all-gather.7.cloned.1.call-update) | async-done | bytes 3932176 | tf_op jit(solution)/shard_map/all_gather | solution.py:247
  847.7 234.7 %while.65 = (s32[]{:T(128)}, bf16[12,1280,64]{1,2,0:T(8,128)(2,1)}, f32[12,1,1024,64]{2,3,1,0:T(8,128)}, f32[12,1,1024]{2,1,0:T(1,128)}, f32[12,1280,64]{1,2,0:T...) while((s32[]{:T(128)}, bf16[12,1280,64]{1,2,0:T(8,128)(2,1)}, ...), condition=%wide.region_28.29_spmd.clone, body=%wide.region_23.28_spmd.sunk.clone | while | flops 2066714880 | bytes 6982853 | solution.py:173
  1101.2 76.7 %reduce-scatter.24.cloned.1.call-done = f32[12,1,64,64]{3,2,1,0:T(8,128)} async-done(((f32[12,1,1024,64]{3,2,1,0:T(8,128)}), f32[12,1,64,64]{3,2,1,0:T(8,128)}) %reduce-scatter.24.cloned.1.call-update) | async-done | bytes 196624 | tf_op jit(solution)/shard_map/reduce_scatter | solution.py:253
  1308.7 9.1 multiply_reduce_fusion.69
  1329.8 7.2 multiply_reduce_fusion.68
  1362.4 27.0 %all_gather.23 = f32[12,1,1024]{0,1,2:T(1,128)} all-gather(f32[12,1,64]{0,1,2:T(1,128)S(1)} %copy.779), channel_id=1, replica_groups=mesh['rows'=16,'hash'=8] {'rows'}, dimensions={2}, use_global_device_ids=true | all-gather | bytes 52224 | tf_op jit(solution)/shard_map/all_gather | solution.py:258
  1391.2 188.8 %while.66 = (s32[]{:T(128)}, bf16[12,1280,64]{1,2,0:T(8,128)(2,1)S(1)}, bf16[12,1280,64]{1,2,0:T(8,128)(2,1)}, f32[12,1280,64]{1,2,0:T(8,128)}, f32[12,1280,64]{...) while((s32[]{:T(128)}, ...), condition=%wide.region_37.38_spmd.clone, body=%wide.region_32.37_spmd.sunk.clone | while | flops 1041729280 | bytes 5676233 | solution.py:157
  1704.9 12.0 convert_reduce_fusion.5
  1726.4 67.0 %all-reduce.65 = (f32[768]{0:T(1024)}, f32[768]{0:T(1024)}, f32[768]{0:T(1024)}, f32[12,65]{0,1:T(8,128)S(1)}, f32[768]{0:T(1024)}, /*index=5*/f32[768]{0:T(1024...) all-reduce(f32[768]{0:T(1024)S(1)} %convert_reduce_fusion.2, ...), channel_id=1, replica_groups=mesh['rows'=16,'hash'=8] {'rows','hash'}, use_global_device_ids=true, to_apply=%region_42.43 | all-reduce | flops 10764 | bytes 86112 | tf_op jit(solution)/shard_map/psum | solution.py:309
  1797.3 165.0 %all-reduce.69.cloned.1.call-done = (f32[768,768]{1,0:T(8,128)}, f32[768,768]{1,0:T(8,128)}, f32[768,768]{1,0:T(8,128)}, f32[768,768]{1,0:T(8,128)}, f32[768,3072]{1,0:T(8,128)}, /*index=5*/f32[3072,768]{1,0:T(8,128)}) async-done(((f32[768,768]{1,0:T(8,128)}, f32[768,768]{1,0:T(8,128)}, f32[768,768]{1,0:T(8,128)}, f32[768,768]{1,0:T(8,128)}, f32[768,3072]{1,0:T(8,128)}, /*index=5*/f32[3072,768]{1,0:T(8,128)}), ...) | async-done | bytes 28311568 | tf_op jit(solution)/shard_map/psum | solution.py:309
  1972.1 9.3 copy.1050
  (2039 shorter events, 1224.3 us)
Async XLA Ops:
  7.2 295.4 %reduce-scatter.28.cloned.1.call-start = ((), (), s32[]{:S(2)}) async-start(), calls=%async_computation.15 | async-start | bytes 3342336
  225.2 145.3 %reduce-scatter.30.cloned.1.call-start = ((), (), s32[]{:S(2)}) async-start(), calls=%async_computation.16 | async-start | bytes 557056
  226.9 433.0 %collective-permute-start = (f32[32,768]{1,0:T(8,128)}, f32[32,768]{1,0:T(8,128)S(1)}, u32[]{:S(2)}, u32[]{:S(2)}) collective-permute-start(f32[32,768]{1,0:T(8,128)} %get-tuple-element.1253), channel_id=1, source_target_pairs={{0,1},{1,2},{2,3},{3,4},{4,5},{5,6},{6,7},{7,8},{8,9},{9,10},{10,1... | collective-permute-start | bytes 294920 | tf_op jit(solution)/shard_map/ppermute | solution.py:21
  231.2 428.6 %collective-permute-start.1 = (f32[32,768]{1,0:T(8,128)}, f32[32,768]{1,0:T(8,128)}, u32[]{:S(2)}, u32[]{:S(2)}) collective-permute-start(f32[32,768]{1,0:T(8,128)} %get-tuple-element.1252), channel_id=1, source_target_pairs={{1,0},{2,1},{3,2},{4,3},{5,4},{6,5},{7,6},{8,7},{9,8},{10,9},{11,1... | collective-permute-start | bytes 294920 | tf_op jit(solution)/shard_map/ppermute | solution.py:22
  248.9 190.8 %all-gather.5.cloned.1.call-start = ((), (), s32[]{:S(2)}) async-start(), calls=%async_computation.9 | async-start | bytes 6684672 | tf_op jit(solution)/shard_map/all_gather | solution.py:192
  249.2 391.7 %copy-start.157 = (f32[160]{0:T(256)}, f32[160]{0:T(256)S(1)}, u32[]{:S(2)}) copy-start(f32[160]{0:T(256)S(1)} %get-tuple-element.1397) | copy-start | bytes 1924
  249.2 392.9 %copy-start.156 = (f32[160]{0:T(256)}, f32[160]{0:T(256)S(1)}, u32[]{:S(2)}) copy-start(f32[160]{0:T(256)S(1)} %get-tuple-element.1396) | copy-start | bytes 1924
  249.3 394.1 %copy-start.155 = (f32[160]{0:T(256)}, f32[160]{0:T(256)S(1)}, u32[]{:S(2)}) copy-start(f32[160]{0:T(256)S(1)} %get-tuple-element.1395) | copy-start | bytes 1924
  249.3 395.2 %copy-start.152 = (f32[160]{0:T(256)}, f32[160]{0:T(256)S(1)}, u32[]{:S(2)}) copy-start(f32[160]{0:T(256)S(1)} %get-tuple-element.1394) | copy-start | bytes 1924
  249.3 396.4 %copy-start.150 = (f32[160]{0:T(256)}, f32[160]{0:T(256)S(1)}, u32[]{:S(2)}) copy-start(f32[160]{0:T(256)S(1)} %get-tuple-element.1393) | copy-start | bytes 1924
  249.3 405.6 %copy-start.148 = (f32[160]{0:T(256)}, f32[160]{0:T(256)S(1)}, u32[]{:S(2)}) copy-start(f32[160]{0:T(256)S(1)} %get-tuple-element.1392) | copy-start | bytes 1924
  258.1 392.1 %copy-start.237 = (f32[160]{0:T(256)}, f32[160]{0:T(256)S(1)}, u32[]{:S(2)}) copy-start(f32[160]{0:T(256)S(1)} %get-tuple-element.1427) | copy-start | bytes 1924
  304.8 353.7 %reduce-scatter.32.cloned.1.call-start = ((), (), s32[]{:S(2)}) async-start(), calls=%async_computation.17 | async-start | bytes 737280
  576.2 123.2 %reduce-scatter.22.cloned.1.call-start = ((), (), s32[]{:S(2)}) async-start(), calls=%async_computation.10 | async-start | bytes 4423680 | tf_op jit(solution)/shard_map/reduce_scatter | solution.py:198
  581.8 257.8 %all-gather.7.cloned.1.call-start = ((), (), s32[]{:S(2)}) async-start(), calls=%async_computation.11 | async-start | bytes 4423680 | tf_op jit(solution)/shard_map/all_gather | solution.py:247
  751.6 426.4 %reduce-scatter.24.cloned.1.call-start = ((), (), s32[]{:S(2)}) async-start(), calls=%async_computation.12 | async-start | bytes 6684672 | tf_op jit(solution)/shard_map/reduce_scatter | solution.py:253
  1088.2 270.9 %reduce-scatter.36.cloned.1.call-start = ((), (), s32[]{:S(2)}) async-start(), calls=%async_computation.19 | async-start | bytes 557056
  1101.2 290.0 %all-gather.9.cloned.1.call-start = ((), (), s32[]{:S(2)}) async-start(), calls=%async_computation.13 | async-start | bytes 6684672 | tf_op jit(solution)/shard_map/all_gather | solution.py:257
  1178.0 523.9 %reduce-scatter.34.cloned.1.call-start = ((), (), s32[]{:S(2)}) async-start(), calls=%async_computation.18 | async-start | bytes 2211840
  1299.8 401.1 %collective-permute-start.2 = (bf16[32,768]{1,0:T(8,128)(2,1)}, bf16[32,768]{1,0:T(8,128)(2,1)}, u32[]{:S(2)}, u32[]{:S(2)}) collective-permute-start(bf16[32,768]{1,0:T(8,128)(2,1)} %get-tuple-element.1259), channel_id=1, source_target_pairs={{0,1},{1,2},{2,3},{3,4},{4,5},{5,6},{6,7},{7,8},{8,9},{9,10},{10,1... | collective-permute-start | bytes 147464 | tf_op jit(solution)/shard_map/ppermute | solution.py:21
  1302.3 398.6 %collective-permute-start.3 = (bf16[32,768]{1,0:T(8,128)(2,1)}, bf16[32,768]{1,0:T(8,128)(2,1)}, u32[]{:S(2)}, u32[]{:S(2)}) collective-permute-start(bf16[32,768]{1,0:T(8,128)(2,1)} %get-tuple-element.1260), channel_id=1, source_target_pairs={{1,0},{2,1},{3,2},{4,3},{5,4},{6,5},{7,6},{8,7},{9,8},{10,9},{11,1... | collective-permute-start | bytes 147464 | tf_op jit(solution)/shard_map/ppermute | solution.py:22
  1359.0 345.9 %reduce-scatter.26.cloned.1.call-start = ((), (), s32[]{:S(2)}) async-start(), calls=%async_computation.14 | async-start | bytes 2211840 | tf_op jit(solution)/shard_map/reduce_scatter | solution.py:269
  1584.1 135.6 %reduce-scatter.38.cloned.1.call-start = ((), (), s32[]{:S(2)}) async-start(), calls=%async_computation.20 | async-start | bytes 2211840
  1623.0 339.3 %all-reduce.69.cloned.1.call-start = ((), (), s32[]{:S(2)}) async-start(), calls=%async_computation.21 | async-start | bytes 56623104 | tf_op jit(solution)/shard_map/psum | solution.py:309
  (400 other events, 8503.5 us)
Sparse Core Ops, SparseCore 0:
  225.3 77.3 reduce-scatter.27
  307.0 63.4 reduce-scatter.29
  373.8 65.9 all-gather.4
  576.3 30.8 reduce-scatter.31
  610.2 89.1 reduce-scatter.21
  751.7 87.7 all-gather.6
  1088.3 89.6 reduce-scatter.23
  1182.2 63.3 reduce-scatter.35
  1248.1 65.5 all-gather.8
  1359.2 48.8 reduce-scatter.33
  1584.3 45.9 reduce-scatter.25
  1632.5 50.2 reduce-scatter.37
  1723.3 239.0 all-reduce.68
where the time goes:
time: 2020 us; the launch traced here: 1990 us
  local copies, waits for them, and re-layouts  677 us (34%)
  matrix products  490 us (24%)
  waiting for transfers between devices  452 us (22%)
  other arithmetic  186 us (9%)
  blocking collectives  145 us (7%)
    psum x1, waiting for transfers between devices, per_device(): lax.psum((grad_w_query, grad_b_query, grad_w_key, grad_b_key, grad_w_valu...  165 us
    unnamed x772, local copies, waits for them, and re-layouts  156 us
    slice x64, local copies, waits for them, and re-layouts, convolve(): shaped[tap_index:tap_index + out_rows]  141 us
    mul x258, local copies, waits for them, and re-layouts, convolve(): taps[:, tap_index][None, :, None] * same_item[:, None, None]  139 us
    dot_general x36, matrix products, read_head(): picked = jnp.einsum('srk,ske->sre', hot, sums_head, precision=HIGHEST)  127 us
    unnamed x19, waiting for transfers between devices  101 us
    dot_general x36, matrix products, read_head(): picked_mass = jnp.einsum('srk,sk->sr', hot, mass_head, precision=HIGHEST)  96 us
    dot_general x24, matrix products, fill_head(): jnp.einsum('srk,sre->ske', hot, key_w[..., None] * value_head[None], prec...  90.7 us
  transfers between devices with their start and end apart: 17, of which 7 were waited for; matrix products, arithmetic and copies ran while one was open for 41% of the time, Pallas kernels for 0%

commit v1 on v0

v1 whole, which is shorter than its diff:
```python
import functools

import jax
import jax.numpy as jnp
from jax import lax
from jax.experimental import pallas as pl
from jax.experimental.pallas import tpu as pltpu
from jax.sharding import Mesh, PartitionSpec as P

BF = jnp.bfloat16
F32 = jnp.float32
HIGHEST = lax.Precision.HIGHEST
EPS_NORM = 1e-05
EPS_UNIT = 1e-06

D = 768
HEADS = 12
HEAD = 64
SETS = 8
BITS = 8
SLOTS = 256
FF = 3072
ROWS = 1280
BLOCK = 2560
OWN = 160
MEMBERS = 16
EDGE = 128
TOTAL = 20480
BLOCKS = 8
MESH = pl.DeviceIdType.MESH
CHUNK = 512
CHUNKS = BLOCK // CHUNK
ITEM = 80
CLASSES = 3
VMEM_LIMIT = 56 * 1024 * 1024

BLOCK_AXES = ("zh", "x")
MEMBER_AXES = ("c", "y", "zl")
ALL_AXES = BLOCK_AXES + MEMBER_AXES


def nt(left, right, **kw):
    return lax.dot_general(left, right, (((1,), (1,)), ((), ())), preferred_element_type=F32, **kw)


def nn(left, right, **kw):
    return lax.dot_general(left, right, (((1,), (0,)), ((), ())), preferred_element_type=F32, **kw)


def tn(left, right, **kw):
    return lax.dot_general(left, right, (((0,), (0,)), ((), ())), preferred_element_type=F32, **kw)


def unit_of(proj):
    scale = lax.rsqrt(jnp.sum(proj * proj, axis=0, keepdims=True) + EPS_UNIT)
    return proj * scale, scale


def bits_of(codes):
    return [(jnp.bitwise_and(codes, 1 << b) != 0) for b in range(BITS)]


def hash_weight(proj, codes, planes):
    unit, _ = unit_of(proj)
    lifted = nn(planes, unit, precision=HIGHEST)
    total = None
    for b, bit in enumerate(bits_of(codes)):
        part = lifted[b * SETS : (b + 1) * SETS]
        part = jnp.where(bit, part, -part)
        total = part if total is None else total + part
    return jnp.exp(total)


def hash_back(z_grad, proj, codes, planes):
    unit, scale = unit_of(proj)
    lifted_grad = jnp.concatenate([jnp.where(bit, z_grad, -z_grad) for bit in bits_of(codes)], axis=0)
    unit_grad = tn(planes, lifted_grad, precision=HIGHEST)
    return scale * (unit_grad - unit * jnp.sum(unit * unit_grad, axis=0, keepdims=True))


def one_hot(codes_row, weight_row):
    width = codes_row.shape[1]
    slots = lax.broadcasted_iota(jnp.int32, (SLOTS, width), 0)
    return jnp.where(slots == codes_row, weight_row, 0.0).astype(BF)


def fill_hot(hot_ref, codes, weights):
    for s in range(SETS):
        hot_ref[s * SLOTS : (s + 1) * SLOTS, :] = one_hot(codes[s : s + 1], weights[s : s + 1])


def by_item(sums, mass, masks):
    width = sums.shape[1]
    lead = lax.broadcasted_iota(jnp.int32, (ITEM - HEAD, width), 0) == 0
    tail = jnp.where(lead, mass, 0.0)
    whole = jnp.concatenate([sums, tail], axis=0)
    return jnp.concatenate([whole * masks[w : w + 1] for w in range(CLASSES)], axis=0).astype(BF)


def pick_item(stacked, masks):
    total = None
    for w in range(CLASSES):
        part = stacked[w * ITEM : (w + 1) * ITEM] * masks[w : w + 1]
        total = part if total is None else total + part
    return total


def circulant(base):
    grid = jnp.broadcast_to(base, (256, 256))
    grid = pltpu.roll(grid, 0, 1, stride=1, stride_axis=0)
    row = lax.broadcasted_iota(jnp.int32, (256, 256), 0)
    col = lax.broadcasted_iota(jnp.int32, (256, 256), 1)
    return (
        jnp.where(col < row, grid, 0.0).astype(BF),
        jnp.where(col >= row, grid, 0.0).astype(BF),
    )


def pack(rows, out, *lead):
    half = OWN // 2
    for p in range(MEMBERS):
        upper = rows[p * OWN : p * OWN + half]
        lower = rows[p * OWN + half : (p + 1) * OWN]
        out[(p, *lead)] = jnp.concatenate([upper, lower], axis=1).astype(BF)


def unpack(chunks, rows):
    half = OWN // 2
    for p in range(MEMBERS):
        both = chunks[p].astype(F32)
        rows[p * OWN : p * OWN + half] = both[:, :HEAD]
        rows[p * OWN + half : (p + 1) * OWN] = both[:, HEAD:]


def chunk_of(i, width=CHUNK, offset=0):
    return pl.ds(pl.multiple_of(i * width, 128) + offset, width)


def fill_kernel(tok, w_t, bias, planes, codes, masks, qkv, weights, long_out, short_out, hot, acc):
    acc[...] = jnp.zeros_like(acc)

    def step(i, _):
        cols = chunk_of(i)
        rows = pl.ds(pl.multiple_of(i * CHUNK, CHUNK), CHUNK)
        proj = nt(w_t[...], tok[rows, :]) + bias[...]
        qkv[:, cols] = proj
        q_codes = codes[0, :, cols]
        k_codes = codes[1, :, cols]
        q_w = hash_weight(proj[:HEAD], q_codes, planes[...])
        k_w = hash_weight(proj[HEAD : 2 * HEAD], k_codes, planes[...])
        weights[:, cols] = jnp.concatenate([q_w, k_w], axis=0)
        items = by_item(proj[2 * HEAD :], jnp.ones((1, CHUNK), F32), masks[:, cols])
        fill_hot(hot, k_codes, k_w)
        acc[...] += nt(items, hot[...])
        return 0

    lax.fori_loop(0, CHUNKS, step, 0)
    long_out[...] = acc[:ITEM].astype(BF)
    short_out[...] = acc[ITEM:].astype(BF)


def read_kernel(
    long_tab, short_tab, codes, weights, masks, value, before, after, v_bias, taps,
    attended, estimate, scale, hot, table, ext, rows_ref,
):
    table[:ITEM] = long_tab[...]
    table[ITEM:] = short_tab[...]
    ones = jnp.ones((1, EDGE), F32)
    ext[:, :EDGE] = by_item(before[...].astype(F32) + v_bias[...], ones, masks[:, :EDGE])
    ext[:, EDGE + BLOCK :] = by_item(after[...].astype(F32) + v_bias[...], ones, masks[:, EDGE + BLOCK :])

    def build(i, _):
        cols = chunk_of(i)
        inner = chunk_of(i, offset=EDGE)
        ext[:, inner] = by_item(value[:, cols] + v_bias[...], jnp.ones((1, CHUNK), F32), masks[:, inner])
        return 0

    lax.fori_loop(0, CHUNKS, build, 0)
    lower, upper = circulant(taps[...])

    def step(i, _):
        cols = chunk_of(i)
        inner = chunk_of(i, offset=EDGE)
        own = masks[:, inner]
        fill_hot(hot, codes[0, :, cols], weights[:SETS, cols])
        found = pick_item(nn(table[...], hot[...]), own)
        recip = 1.0 / (found[HEAD : HEAD + 1] + 1.0)
        est = (found[:HEAD] - v_bias[...]) * recip
        estimate[:, cols] = est
        scale[:, cols] = recip
        mixed = []
        for half in range(2):
            at = pl.multiple_of(i * CHUNK, 256) + half * 256
            mixed.append(nn(ext[:, pl.ds(at, 256)], lower) + nn(ext[:, pl.ds(at + 256, 256)], upper))
        conv = pick_item(jnp.concatenate(mixed, axis=1), own)[:HEAD]
        rows = pl.ds(pl.multiple_of(i * CHUNK, CHUNK), CHUNK)
        rows_ref[rows, :] = jnp.transpose(est + v_bias[...] + conv)
        return 0

    lax.fori_loop(0, CHUNKS, step, 0)
    pack(rows_ref, attended)


def read_back_kernel(
    chunks, estimate, scale, codes, weights, masks, long_out, short_out, grad, denom, hot, acc,
    grad_rows,
):
    acc[...] = jnp.zeros_like(acc)
    unpack(chunks, grad_rows)

    def step(i, _):
        cols = chunk_of(i)
        rows = pl.ds(pl.multiple_of(i * CHUNK, CHUNK), CHUNK)
        got = jnp.transpose(grad_rows[rows, :])
        grad[:, cols] = got
        numer = got * scale[:, cols]
        den = -jnp.sum(numer * estimate[:, cols], axis=0, keepdims=True)
        denom[:, cols] = den
        items = by_item(numer, den, masks[:, cols])
        fill_hot(hot, codes[0, :, cols], weights[:SETS, cols])
        acc[...] += nt(items, hot[...])
        return 0

    lax.fori_loop(0, CHUNKS, step, 0)
    long_out[...] = acc[:ITEM].astype(BF)
    short_out[...] = acc[ITEM:].astype(BF)


def query_back_kernel(
    long_tab, short_tab, grad, denom, scale, codes, weights, masks, query, planes, out, table
):
    table[:ITEM] = long_tab[...]
    table[ITEM:] = short_tab[...]

    def step(i, _):
        cols = chunk_of(i)
        own = masks[:, cols]
        q_codes = codes[0, :, cols]
        numer = grad[:, cols] * scale[:, cols]
        den = denom[:, cols]
        parts = []
        for s in range(SETS):
            hot = one_hot(q_codes[s : s + 1], 1.0)
            found = pick_item(nn(table[:, s * SLOTS : (s + 1) * SLOTS], hot), own)
            parts.append(
                jnp.sum(found[:HEAD] * numer, axis=0, keepdims=True) + found[HEAD : HEAD + 1] * den
            )
        z_grad = jnp.concatenate(parts, axis=0) * weights[:SETS, cols]
        out[:, cols] = hash_back(z_grad, query[:, cols], q_codes, planes[...]).astype(BF)
        return 0

    lax.fori_loop(0, CHUNKS, step, 0)


def key_back_kernel(
    long_tab, short_tab, grad, before, after, codes, weights, masks, qkv, v_before, v_after,
    planes, v_bias, taps_back, q_grad, tok,
    grad_out, w_out, b_out, taps_out, table, ext, v_ext, g_all, rows_ref,
):
    table[:ITEM] = long_tab[...]
    table[ITEM:] = short_tab[...]
    none = jnp.zeros((1, EDGE), F32)
    lo, hi = slice(None, EDGE), slice(EDGE + BLOCK, None)
    ext[:, lo] = by_item(before[...].astype(F32), none, masks[:, lo])
    ext[:, hi] = by_item(after[...].astype(F32), none, masks[:, hi])
    v_ext[:, lo] = by_item(v_before[...].astype(F32) + v_bias[...], none, masks[:, lo])
    v_ext[:, hi] = by_item(v_after[...].astype(F32) + v_bias[...], none, masks[:, hi])

    def build(i, _):
        cols = chunk_of(i)
        inner = chunk_of(i, offset=EDGE)
        zero = jnp.zeros((1, CHUNK), F32)
        ext[:, inner] = by_item(grad[:, cols], zero, masks[:, inner])
        v_ext[:, inner] = by_item(qkv[2 * HEAD :, cols] + v_bias[...], zero, masks[:, inner])
        return 0

    lax.fori_loop(0, CHUNKS, build, 0)
    lower, upper = circulant(taps_back[...])

    def step(i, carry):
        cols = chunk_of(i)
        inner = chunk_of(i, offset=EDGE)
        own = masks[:, inner]
        k_codes = codes[1, :, cols]
        k_w = weights[SETS:, cols]
        val = qkv[2 * HEAD :, cols]
        parts = []
        v_grad = jnp.zeros((HEAD, CHUNK), F32)
        for s in range(SETS):
            hot = one_hot(k_codes[s : s + 1], 1.0)
            found = pick_item(nn(table[:, s * SLOTS : (s + 1) * SLOTS], hot), own)
            parts.append(
                jnp.sum(found[:HEAD] * val, axis=0, keepdims=True) + found[HEAD : HEAD + 1]
            )
            v_grad = v_grad + found[:HEAD] * k_w[s : s + 1]
        z_grad = jnp.concatenate(parts, axis=0) * k_w
        k_grad = hash_back(z_grad, qkv[HEAD : 2 * HEAD, cols], k_codes, planes[...])
        mixed = []
        c_low, c_high = carry
        for half in range(2):
            at = pl.multiple_of(i * CHUNK, 256) + half * 256
            mixed.append(nn(ext[:, pl.ds(at, 256)], lower) + nn(ext[:, pl.ds(at + 256, 256)], upper))
            here = ext[:, pl.ds(at + EDGE, 256)]
            c_low = c_low + tn(v_ext[:, pl.ds(at, 256)], here)
            c_high = c_high + tn(v_ext[:, pl.ds(at + 256, 256)], here)
        v_grad = v_grad + pick_item(jnp.concatenate(mixed, axis=1), own)[:HEAD]
        g_all[:HEAD, cols] = q_grad[:, cols]
        g_all[HEAD : 2 * HEAD, cols] = k_grad.astype(BF)
        g_all[2 * HEAD :, cols] = v_grad.astype(BF)
        return c_low, c_high

    zeros = jnp.zeros((256, 256), F32)
    c_low, c_high = lax.fori_loop(0, CHUNKS, step, (zeros, zeros))
    row = lax.broadcasted_iota(jnp.int32, (256, 256), 0)
    col = lax.broadcasted_iota(jnp.int32, (256, 256), 1)
    skew = jnp.where(col < row, c_low, c_high)
    for b in range(8):
        skew = jnp.where(jnp.bitwise_and(row, 1 << b) != 0, pltpu.roll(skew, 256 - (1 << b), 1), skew)
    taps_out[...] = jnp.sum(skew, axis=0, keepdims=True)
    for k in range(3):
        rows_ref[...] = jnp.transpose(g_all[k * HEAD : (k + 1) * HEAD, :].astype(F32))
        pack(rows_ref, grad_out, k)
    w_out[...] = nn(g_all[...], tok[...])
    b_out[...] = jnp.sum(g_all[...].astype(F32), axis=1, keepdims=True)


def member_id(member):
    return {"c": member // 8, "y": (member % 8) // 2, "zl": member % 2}


def block_id(block):
    return {"zh": block // 4, "x": block % 4}


def my_member():
    return lax.axis_index("c") * 8 + lax.axis_index("y") * 2 + lax.axis_index("zl")


def my_block():
    return lax.axis_index("zh") * 4 + lax.axis_index("x")


def greet(ids):
    barrier = pltpu.get_barrier_semaphore()
    for one in ids:
        pl.semaphore_signal(barrier, inc=1, device_id=one, device_id_type=MESH)
    pl.semaphore_wait(barrier, len(ids))


def send(src, dst, send_sem, recv_sem, device):
    return pltpu.make_async_remote_copy(
        src_ref=src, dst_ref=dst, send_sem=send_sem, recv_sem=recv_sem,
        device_id=device, device_id_type=MESH,
    )


def start_kernel(tokens, both, planes, tok_out, codes_out, planes_out, local, send_sem, recv_sem):
    me = my_member()
    core = lax.axis_index("c")
    mine = me % 8
    greet([member_id((me + d) % MEMBERS) for d in range(1, MEMBERS)])
    part = pl.ds(pl.multiple_of(core * ROWS, ROWS), ROWS)
    swap = send(tokens, tok_out.at[part], send_sem.at[32], recv_sem.at[32], member_id((me + 8) % MEMBERS))
    swap.start()
    keep = pltpu.make_async_copy(tokens, tok_out.at[part], local.at[0])
    keep.start()

    def codes_to(d):
        to = (me + d) % MEMBERS
        return to, send(
            both.at[jnp.minimum(to, HEADS - 1)], codes_out.at[me], send_sem.at[d],
            recv_sem.at[me], member_id(to),
        )

    def planes_to(d):
        to = core * 8 + (mine + d) % 8
        return send(planes, planes_out.at[mine], send_sem.at[16 + d], recv_sem.at[16 + mine], member_id(to))

    for d in range(1, MEMBERS):
        to, copy = codes_to(d)
        pl.when(to < HEADS)(copy.start)
    for d in range(1, 8):
        planes_to(d).start()
    own_codes = pltpu.make_async_copy(both.at[jnp.minimum(me, HEADS - 1)], codes_out.at[me], local.at[1])
    own_codes.start()
    own_planes = pltpu.make_async_copy(planes, planes_out.at[mine], local.at[2])
    own_planes.start()
    keep.wait()
    own_codes.wait()
    own_planes.wait()
    for d in range(1, MEMBERS):
        to, copy = codes_to(d)
        pl.when(to < HEADS)(copy.wait_send)
        came = (me + d) % MEMBERS
        got = send(both.at[0], codes_out.at[came], send_sem.at[d], recv_sem.at[came], member_id(came))
        pl.when(me < HEADS)(got.wait_recv)
    for d in range(1, 8):
        planes_to(d).wait_send()
        came = (mine + d) % 8
        send(
            planes, planes_out.at[came], send_sem.at[16 + d], recv_sem.at[16 + came],
            member_id(core * 8 + came),
        ).wait_recv()
    swap.wait_send()
    other = pl.ds(pl.multiple_of((1 - core) * ROWS, ROWS), ROWS)
    send(tokens, tok_out.at[other], send_sem.at[32], recv_sem.at[32], member_id((me + 8) % MEMBERS)).wait_recv()


def scatter_kernel(chunks, out, local, send_sem, recv_sem):
    me = my_member()
    greet([member_id((me + d) % MEMBERS) for d in range(1, MEMBERS)])
    owner = me < HEADS
    mine = jnp.minimum(me, HEADS - 1)

    def to(d):
        dest = (me + d) % MEMBERS
        return send(chunks.at[dest], out.at[mine], send_sem.at[d], recv_sem.at[mine], member_id(dest))

    for d in range(1, MEMBERS):
        pl.when(owner)(to(d).start)
    keep = pltpu.make_async_copy(chunks.at[me], out.at[mine], local)
    pl.when(owner)(keep.start)
    for h in range(HEADS):
        got = send(chunks.at[0], out.at[h], send_sem.at[0], recv_sem.at[h], member_id(h))
        pl.when(me != h)(got.wait_recv)
    for d in range(1, MEMBERS):
        pl.when(owner)(to(d).wait_send)
    pl.when(owner)(keep.wait)


def gather_kernel(chunks, out, local, send_sem, recv_sem):
    me = my_member()
    greet([member_id((me + d) % MEMBERS) for d in range(1, MEMBERS)])
    owner = me < HEADS
    mine = jnp.minimum(me, HEADS - 1)

    def to(d):
        dest = (me + d) % MEMBERS
        copy = send(
            chunks.at[jnp.minimum(dest, HEADS - 1)], out.at[me], send_sem.at[d], recv_sem.at[me],
            member_id(dest),
        )
        return dest < HEADS, copy

    for d in range(1, MEMBERS):
        wanted, copy = to(d)
        pl.when(wanted)(copy.start)
    keep = pltpu.make_async_copy(chunks.at[mine], out.at[me], local)
    keep.start()
    for d in range(1, MEMBERS):
        came = (me + d) % MEMBERS
        got = send(chunks.at[0], out.at[came], send_sem.at[0], recv_sem.at[came], member_id(came))
        pl.when(owner)(got.wait_recv)
    for d in range(1, MEMBERS):
        wanted, copy = to(d)
        pl.when(wanted)(copy.wait_send)
    keep.wait()


def reduce_kernel(part, first, last, out, before, after, got, send_sem, recv_sem, halo_send, halo_recv):
    me = my_block()
    greet([block_id((me + d) % BLOCKS) for d in range(1, BLOCKS)])
    down, up = block_id((me + BLOCKS - 1) % BLOCKS), block_id((me + 1) % BLOCKS)

    def cols(k):
        return pl.ds(pl.multiple_of(k * SLOTS, SLOTS), SLOTS)

    def to_share(d):
        dest = (me + d) % BLOCKS
        return send(
            part.at[:, cols(dest)], got.at[d], send_sem.at[d], recv_sem.at[d], block_id(dest)
        )

    for d in range(1, BLOCKS):
        to_share(d).start()
    to_down = send(first, after, halo_send.at[0], halo_recv.at[0], down)
    to_up = send(last, before, halo_send.at[1], halo_recv.at[1], up)
    to_down.start()
    to_up.start()
    total = part[:, cols(me)].astype(F32)
    for d in range(1, BLOCKS):
        to_share(d).wait_recv()
        total = total + got[d].astype(F32)
    out[:, cols(me)] = total.astype(BF)

    def to_all(d):
        dest = (me + d) % BLOCKS
        return send(
            out.at[:, cols(me)], out.at[:, cols(me)], send_sem.at[BLOCKS + d], recv_sem.at[BLOCKS + d],
            block_id(dest),
        )

    for d in range(1, BLOCKS):
        to_all(d).start()
    for d in range(1, BLOCKS):
        came = (me + BLOCKS - d) % BLOCKS
        send(
            out.at[:, cols(came)], out.at[:, cols(came)], send_sem.at[BLOCKS + d],
            recv_sem.at[BLOCKS + d], block_id(came),
        ).wait_recv()
        to_share(d).wait_send()
        to_all(d).wait_send()
    to_down.wait()
    to_up.wait()


def call(kernel, outs, scratch, *args):
    return pl.pallas_call(
        kernel,
        out_shape=[jax.ShapeDtypeStruct(shape, kind) for shape, kind in outs],
        in_specs=[pl.BlockSpec(memory_space=pltpu.VMEM)] * len(args),
        out_specs=[pl.BlockSpec(memory_space=pltpu.VMEM)] * len(outs),
        scratch_shapes=[pltpu.VMEM(shape, kind) for shape, kind in scratch],
        compiler_params=pltpu.CompilerParams(vmem_limit_bytes=VMEM_LIMIT),
    )(*args)


def talk(kernel, ident, outs, scratch, *args):
    return pl.pallas_call(
        kernel,
        out_shape=[jax.ShapeDtypeStruct(shape, kind) for shape, kind in outs],
        in_specs=[pl.BlockSpec(memory_space=pltpu.VMEM)] * len(args),
        out_specs=[pl.BlockSpec(memory_space=pltpu.VMEM)] * len(outs),
        scratch_shapes=scratch,
        compiler_params=pltpu.CompilerParams(
            collective_id=ident, has_side_effects=True, vmem_limit_bytes=VMEM_LIMIT
        ),
    )(*args)


def dma(count):
    return pltpu.SemaphoreType.DMA((count,))


def all_to_members(array, ident):
    shape = (HEADS,) + array.shape[1:]
    (out,) = talk(scatter_kernel, ident, [(shape, BF)], [pltpu.SemaphoreType.DMA, dma(16), dma(16)], array)
    return out


def all_to_owners(array, ident):
    shape = (MEMBERS,) + array.shape[1:]
    (out,) = talk(gather_kernel, ident, [(shape, BF)], [pltpu.SemaphoreType.DMA, dma(16), dma(16)], array)
    return out


def sum_blocks(part, first, last, ident):
    edge = ((HEAD, EDGE), BF)
    return talk(
        reduce_kernel, ident, [((ITEM, SETS * SLOTS), BF), edge, edge],
        [pltpu.VMEM((BLOCKS, ITEM, SLOTS), BF), dma(2 * BLOCKS), dma(2 * BLOCKS), dma(2), dma(2)],
        part, first, last,
    )


def layer_norm(values, norm_gain, norm_bias):
    row_mean = jnp.mean(values, axis=-1, keepdims=True)
    centred = values - row_mean
    spread = jnp.mean(centred * centred, axis=-1, keepdims=True)
    return centred * lax.rsqrt(spread + EPS_NORM) * norm_gain + norm_bias


def gelu_exact(values):
    return jax.nn.gelu(values, approximate=False)


def to_members(array):
    return lax.all_to_all(array, MEMBER_AXES, 0, 0, tiled=True)


def from_neighbours(first, last):
    up = [(i, (i + 1) % 8) for i in range(8)]
    down = [(j, i) for i, j in up]
    return lax.ppermute(last, BLOCK_AXES, up), lax.ppermute(first, BLOCK_AXES, down)


def item_masks(cuts, block):
    start = block * BLOCK - EDGE
    pos = start + jnp.arange(BLOCK + 2 * EDGE, dtype=jnp.int32)
    item = jnp.sum((pos[None, :] >= cuts[:, None]).astype(jnp.int32), axis=0) - 1
    longest = jnp.where(cuts[2] - cuts[1] > 1024, 1, 2)
    first_half = block < 4
    outer = jnp.where(first_half, 0, 3)
    inner = jnp.where(first_half, 1, 2)
    valid = (pos >= 0) & (pos < TOTAL)
    is_long = valid & (item == longest)
    is_outer = valid & (item == outer)
    is_inner = valid & (item == inner) & (inner != longest)
    none = jnp.zeros_like(is_long)
    return jnp.stack([is_long, is_outer, is_inner] + [none] * 5).astype(F32)


def per_device(
    tokens, item_cuts, q_codes, k_codes, hyperplanes, w_query, b_query, w_key, b_key,
    w_value, b_value, conv_weight, w_out, b_out, ln1_gain, ln1_bias, w_in, b_in, w_back,
    b_back, ln2_gain, ln2_bias, cotangent,
):
    block = lax.axis_index(BLOCK_AXES)
    member = lax.axis_index(MEMBER_AXES)
    hash_at = lax.axis_index(("y", "zl"))
    head = jnp.minimum(member, HEADS - 1)
    both = jnp.concatenate([q_codes, k_codes], axis=0).transpose(1, 0, 2)
    tok, both, planes = talk(
        start_kernel, 0,
        [((BLOCK, D), BF), ((MEMBERS, 2, ROWS), jnp.int32), ((SETS, BITS, HEAD), F32)],
        [dma(3), dma(33), dma(33)],
        tokens, both, hyperplanes[0].T,
    )
    codes = both.reshape(2, SETS, 2, ROWS).transpose(2, 1, 0, 3).reshape(2, SETS, BLOCK)
    planes = planes.transpose(1, 0, 2).reshape(BITS * SETS, HEAD)
    masks = item_masks(item_cuts, block)
    own_masks = masks[:, EDGE : EDGE + BLOCK]

    def head_cols(weight):
        return lax.dynamic_slice_in_dim(weight, head * HEAD, HEAD, 1).T

    def head_bias(bias):
        return lax.dynamic_slice_in_dim(bias, head * HEAD, HEAD, 0)[:, None]

    w_t = jnp.concatenate([head_cols(w) for w in (w_query, w_key, w_value)], axis=0)
    v_bias = head_bias(b_value)
    bias_t = jnp.concatenate([head_bias(b_query), head_bias(b_key), jnp.zeros_like(v_bias)], axis=0)
    taps = lax.dynamic_slice_in_dim(conv_weight, head, 1, 0)
    taps_fwd = jnp.pad(taps[:, ::-1], ((0, 0), (96, 95)))
    taps_bwd = jnp.pad(taps, ((0, 0), (96, 95)))

    hot = ((SETS * SLOTS, CHUNK), BF)
    acc = ((CLASSES * ITEM, SETS * SLOTS), F32)
    table = ((CLASSES * ITEM, SETS * SLOTS), BF)
    ext = ((CLASSES * ITEM, BLOCK + 2 * EDGE), BF)
    rows_f32 = ((BLOCK, HEAD), F32)
    long_shape = ((ITEM, SETS * SLOTS), BF)
    short_shape = (((CLASSES - 1) * ITEM, SETS * SLOTS), BF)

    qkv, weights, long_part, short_tab = call(
        fill_kernel,
        [((3 * HEAD, BLOCK), F32), ((2 * SETS, BLOCK), F32), long_shape, short_shape],
        [hot, acc],
        tok, w_t, bias_t, planes, codes, own_masks,
    )
    value = qkv[2 * HEAD :]
    long_tab, v_before, v_after = sum_blocks(
        long_part, value[:, :EDGE].astype(BF), value[:, -EDGE:].astype(BF), 1
    )
    att_rows, estimate, scale = call(
        read_kernel,
        [((MEMBERS, OWN // 2, 2 * HEAD), BF), ((HEAD, BLOCK), F32), ((1, BLOCK), F32)],
        [hot, table, ext, rows_f32],
        long_tab, short_tab, codes, weights, masks, value, v_before, v_after, v_bias, taps_fwd,
    )
    att = all_to_members(att_rows, 2)
    attended_low = att.reshape(HEADS, OWN // 2, 2, HEAD).transpose(2, 1, 0, 3).reshape(OWN, D)

    own_tokens = lax.dynamic_slice_in_dim(tokens, hash_at * OWN, OWN, 0)
    branch = nn(attended_low, w_out) + b_out
    hidden, norm_one_back = jax.vjp(layer_norm, own_tokens.astype(F32) + branch, ln1_gain, ln1_bias)
    hidden_low = hidden.astype(BF)
    inner_pre = nn(hidden_low, w_in) + b_in
    activated, gelu_back = jax.vjp(gelu_exact, inner_pre)
    activated_low = activated.astype(BF)
    outer_out = nn(activated_low, w_back) + b_back
    output, norm_two_back = jax.vjp(layer_norm, hidden + outer_out, ln2_gain, ln2_bias)
    sum_grad, grad_ln2_gain, grad_ln2_bias = norm_two_back(cotangent)
    outer_grad = sum_grad.astype(BF)
    grad_w_back = tn(activated_low, outer_grad)
    grad_b_back = jnp.sum(outer_grad.astype(F32), axis=0)
    (inner_grad,) = gelu_back(nt(outer_grad, w_back))
    inner_low = inner_grad.astype(BF)
    grad_w_in = tn(hidden_low, inner_low)
    grad_b_in = jnp.sum(inner_low.astype(F32), axis=0)
    hidden_grad = sum_grad + nt(inner_low, w_in)
    resid_grad, grad_ln1_gain, grad_ln1_bias = norm_one_back(hidden_grad)
    branch_grad = resid_grad.astype(BF)
    grad_w_out = tn(attended_low, branch_grad)
    grad_b_out = jnp.sum(branch_grad.astype(F32), axis=0)
    attended_grad = nt(branch_grad, w_out).astype(BF)

    grad_chunks = attended_grad.reshape(2, OWN // 2, HEADS, HEAD).transpose(2, 1, 0, 3)
    grad_rows = all_to_owners(grad_chunks.reshape(HEADS, OWN // 2, 2 * HEAD), 3)
    long_gpart, short_gtab, grad_t, denom = call(
        read_back_kernel,
        [long_shape, short_shape, ((HEAD, BLOCK), F32), ((1, BLOCK), F32)],
        [hot, acc, rows_f32],
        grad_rows, estimate, scale, codes, weights, own_masks,
    )
    long_gtab, g_before, g_after = sum_blocks(
        long_gpart, grad_t[:, :EDGE].astype(BF), grad_t[:, -EDGE:].astype(BF), 1
    )
    (q_grad,) = call(
        query_back_kernel,
        [((HEAD, BLOCK), BF)],
        [table],
        long_tab, short_tab, grad_t, denom, scale, codes, weights, own_masks, qkv[:HEAD], planes,
    )
    grad_qkv, head_w, head_b, head_taps = call(
        key_back_kernel,
        [((MEMBERS, 3, OWN // 2, 2 * HEAD), BF), ((3 * HEAD, D), F32), ((3 * HEAD, 1), F32), ((1, 256), F32)],
        [table, ext, ext, ((3 * HEAD, BLOCK), BF), rows_f32],
        long_gtab, short_gtab, grad_t, g_before, g_after, codes, weights, masks, qkv,
        v_before, v_after, planes, v_bias, taps_bwd, q_grad, tok,
    )

    lows = all_to_members(grad_qkv, 4)
    lows = lows.reshape(HEADS, 3, OWN // 2, 2, HEAD).transpose(1, 3, 2, 0, 4).reshape(3, OWN, D)
    grad_tokens = resid_grad + nt(lows[0], w_query) + nt(lows[1], w_key) + nt(lows[2], w_value)

    def all_heads(array):
        return lax.all_gather(lax.psum(array, BLOCK_AXES), MEMBER_AXES, axis=0)[:HEADS]

    heads_w = all_heads(head_w.astype(BF)).astype(F32).reshape(HEADS, 3, HEAD, D)
    heads_w = heads_w.transpose(1, 3, 0, 2).reshape(3, D, D)
    small = jnp.concatenate([head_b[:, 0], head_taps[0, 96:161][::-1]])
    heads_small = all_heads(small)
    heads_b = heads_small[:, : 3 * HEAD].reshape(HEADS, 3, HEAD).transpose(1, 0, 2).reshape(3, D)
    grad_conv_weight = heads_small[:, 3 * HEAD :]

    grad_w_in, grad_w_back, grad_w_out = [
        part.astype(F32)
        for part in lax.psum(
            (grad_w_in.astype(BF), grad_w_back.astype(BF), grad_w_out.astype(BF)), ALL_AXES
        )
    ]
    vectors = (
        grad_b_out, grad_ln1_gain, grad_ln1_bias, grad_b_back, grad_ln2_gain, grad_ln2_bias, grad_b_in,
    )
    joined = lax.psum(jnp.concatenate(vectors), ALL_AXES)
    (
        grad_b_out, grad_ln1_gain, grad_ln1_bias, grad_b_back, grad_ln2_gain, grad_ln2_bias, grad_b_in,
    ) = jnp.split(joined, [D * (k + 1) for k in range(6)])
    return (
        output, grad_tokens, heads_w[0], heads_b[0], heads_w[1], heads_b[1], heads_w[2], heads_b[2],
        grad_conv_weight, grad_w_out, grad_b_out, grad_ln1_gain, grad_ln1_bias, grad_w_in, grad_b_in,
        grad_w_back, grad_b_back, grad_ln2_gain, grad_ln2_bias,
    )


def solution(mesh):
    grid = Mesh(mesh.devices.reshape(2, 4, 2, 4, 2), ALL_AXES)
    rows = ("zh", "x", "c")
    sets = ("y", "zl")
    placed = (
        P(rows, None), P(), P(sets, None, rows), P(sets, None, rows), P(sets, None, None),
    ) + (P(),) * 17 + (P(ALL_AXES, None),)
    return jax.shard_map(
        per_device,
        mesh=grid,
        in_specs=placed,
        out_specs=(P(ALL_AXES, None), P(ALL_AXES, None)) + (P(),) * 17,
        check_vma=False,
    )
```

time: 2020 us -> 496 us (0.25); the launches traced: 1990 us -> 495 us
  local copies, waits for them, and re-layouts: 677 us -> 46.8 us
  matrix products: 490 us -> 28.2 us
  waiting for transfers between devices: 452 us -> 120 us
  other arithmetic: 186 us -> 27.1 us
  Pallas kernels: 0 us -> 138 us
  blocking collectives: 145 us -> 118 us
    dot_general x210 -> x12, matrix products: 490 us -> 28.2 us  [the longest x6 9.74 us: nt(): lax.dot_general(left, right, (((1,), (1,)), ((), ())), preferred_element_...]
    unnamed x772 -> x95, local copies, waits for them, and re-layouts: 156 us -> 10.3 us
    squeeze x120 -> x7, local copies, waits for them, and re-layouts: 148 us -> 5.26 us  [the longest x1 2.04 us: per_device(): lows[0]]
    mul x284 -> x0, local copies, waits for them, and re-layouts: 139 us -> none  [the longest x258 139 us: convolve(): taps[:, tap_index][None, :, None] * same_item[:, None, None]]
    pallas_call x0 -> x11, Pallas kernels: none -> 138 us  [the longest x6 87.7 us: talk(): pl.pallas_call(kernel, out_shape=[jax.ShapeDtypeStruct(shape, kind) for s...]
    slice x71 -> x15, local copies, waits for them, and re-layouts: 147 us -> 13.7 us  [the longest x1 2.64 us: per_device(): heads_w[2]]
    reduce_sum x93 -> x3, other arithmetic: 131 us -> 2.18 us  [the longest x1 0.76 us: item_masks(): jnp.sum((pos[None, :] >= cuts[:, None]).astype(jnp.int32), axis=0) - 1]
    reduce_scatter x3 -> x0, waiting for transfers between devices: 116 us -> none  [the longest x1 76.7 us: per_device(): lax.psum_scatter(placed_sums_grad, 'rows', scatter_dimension=2, tiled=True)]
  transfers between devices with their start and end apart: 17 -> 3, of which waited for: 7 -> 3; matrix products, arithmetic and copies ran while one was open for 41% -> 8% of each run, Pallas kernels for 0% -> 4%
where the time goes in v1:
time: 496 us; the launch traced here: 495 us
  Pallas kernels  138 us (28%)
  waiting for transfers between devices  120 us (24%)
  blocking collectives  118 us (24%)
  local copies, waits for them, and re-layouts  46.8 us (9%)
  matrix products  28.2 us (6%)
  other arithmetic  27.1 us (5%)
  between operations  15.9 us (3%)
    pallas_call x6, Pallas kernels, talk(): pl.pallas_call(kernel, out_shape=[jax.ShapeDtypeStruct(shape, kind) for s...  87.7 us
    psum x1, waiting for transfers between devices, all_heads(): lax.psum(array, BLOCK_AXES)  72.3 us
    psum x1, blocking collectives, per_device(): joined = lax.psum(jnp.concatenate(vectors), ALL_AXES)  62.6 us
    pallas_call x5, Pallas kernels, call(): pl.pallas_call(kernel, out_shape=[jax.ShapeDtypeStruct(shape, kind) for s...  50 us
    all_gather x1, blocking collectives, all_heads(): lax.all_gather(lax.psum(array, BLOCK_AXES), MEMBER_AXES, axis=0)[:HEADS]  38.3 us
    psum x1, waiting for transfers between devices, per_device(): lax.psum((grad_w_in.astype(BF), grad_w_back.astype(BF), grad_w_out.astype...  24 us
    all_gather x1, waiting for transfers between devices, all_heads(): lax.all_gather(lax.psum(array, BLOCK_AXES), MEMBER_AXES, axis=0)[:HEADS]  24 us
    psum x1, blocking collectives, all_heads(): lax.psum(array, BLOCK_AXES)  17.5 us
  transfers between devices with their start and end apart: 3, of which 3 were waited for; matrix products, arithmetic and copies ran while one was open for 8% of the time, Pallas kernels for 4%

profile of v1, /device:TPU:1, one launch (start us, length us, event | category | flops | bytes accessed | tf_op | source)
XLA Modules:
  0.0 494.6 jit_solution(12009134236371998065)
XLA Ops:
  19.0 13.8 %shard_map.366 = (bf16[2560,768]{1,0:T(8,128)(2,1)}, s32[16,2,1280]{2,1,0:T(2,128)}, f32[8,8,64]{2,1,0:T(8,128)}) custom-call(bf16[1280,768]{1,0:T(8,128)(2,1)} %tokens.1, s32[12,2,1280]{2,1,0:T(2,128)} %add_bitcast_fusion.both, f32[8,64]{1,0:T(8,128)} %bitcast.111), custom_call_target="tpu_custom_call" | custom-call | tf_op jit(solution)/shard_map/pallas_call | solution.py:519
  36.5 11.2 %shard_map.367 = (f32[192,2560]{1,0:T(8,128)}, f32[16,2560]{1,0:T(8,128)}, bf16[80,2048]{1,0:T(8,128)(2,1)}, bf16[160,2048]{1,0:T(8,128)(2,1)}) custom-call(bf16[2560,768]{1,0:T(8,128)(2,1)} %get-tuple-element.43.tok, bf16[192,768]{1,0:T(8,128)(2,1)} %pad_maximum_fusion.w_t, f32[192,1]{1,0:T(8,128)} %copy.122.bias, f32[64,64]{1,0:T(8,128)} %bitcast.99, ...), custom_call_target="tpu_custom_call" | custom-call | tf_op jit(solution)/shard_map/pallas_call | solution.py:508
  52.9 19.1 %shard_map.368 = (bf16[80,2048]{1,0:T(8,128)(2,1)}, bf16[64,128]{1,0:T(8,128)(2,1)}, bf16[64,128]{1,0:T(8,128)(2,1)}) custom-call(bf16[80,2048]{1,0:T(8,128)(2,1)} %get-tuple-element.46.part, bf16[64,128]{1,0:T(8,128)(2,1)} %get-tuple-element.176.first, bf16[64,128]{1,0:T(8,128)(2,1)} %get-tuple-element.175.last), custom_call_target="tpu_custom_call" | custom-call | tf_op jit(solution)/shard_map/pallas_call | solution.py:519
  72.0 8.0 %shard_map.369 = (bf16[16,80,128]{2,1,0:T(8,128)(2,1)}, f32[64,2560]{1,0:T(8,128)}, f32[1,2560]{1,0:T(1,128)}) custom-call(bf16[80,2048]{1,0:T(8,128)(2,1)} %get-tuple-element.48.long_tab, bf16[160,2048]{1,0:T(8,128)(2,1)} %get-tuple-element.49.short_tab, s32[2,8,2560]{2,1,0:T(8,128)} %bitcast.85, f32[16,2560]{1,0:T(8,128)} %get-tuple-element.50.weights, ...), custom_call_target="tpu_custom_call" | custom-call | tf_op jit(solution)/shard_map/pallas_call | solution.py:508
  80.0 10.6 %shard_map.370 = bf16[12,80,128]{2,1,0:T(8,128)(2,1)} custom-call(bf16[16,80,128]{2,1,0:T(8,128)(2,1)} %get-tuple-element.53.chunks), custom_call_target="tpu_custom_call" | custom-call | tf_op jit(solution)/shard_map/pallas_call | solution.py:519
  94.3 7.0 %multiply_convert_fusion = (bf16[160,3072]{1,0:T(8,128)(2,1)S(1)}, f32[160,3072]{1,0:T(8,128)S(1)}, f32[160,3072]{1,0:T(8,128)S(1)}) fusion(f32[3072]{0:T(1024)S(1)} %copy-done.33, bf16[768,3072]{1,0:T(8,128)(2,1)} %param.39, f32[160,768]{1,0:T(8,128)S(1)} %get-tuple-element.192, f32[768]{0:T(1024)S(1)} %copy-done.16, f32[768]{0:T(1024)S(1)} %copy-done.15, ...), kind=kOutput, calls=%fused_computation.8 | convolution fusion | flops 788029440 | bytes 10145024 | tf_op jit(solution)/shard_map/dot_general | solution.py:47
  116.1 10.2 %shard_map.371.chunks = bf16[16,80,128]{2,1,0:T(8,128)(2,1)} custom-call(bf16[12,80,128]{2,1,0:T(8,128)(2,1)} %copy.128.chunks), custom_call_target="tpu_custom_call" | custom-call | tf_op jit(solution)/shard_map/pallas_call | solution.py:519
  126.2 6.7 %shard_map.372 = (bf16[80,2048]{1,0:T(8,128)(2,1)}, bf16[160,2048]{1,0:T(8,128)(2,1)}, f32[64,2560]{1,0:T(8,128)}, f32[1,2560]{1,0:T(1,128)}) custom-call(bf16[16,80,128]{2,1,0:T(8,128)(2,1)} %shard_map.371.chunks, f32[64,2560]{1,0:T(8,128)} %get-tuple-element.54.estimate, f32[1,2560]{1,0:T(1,128)} %get-tuple-element.55.scale, s32[2,8,2560]{2,1,0:T(8,128)} %bitcast.86, ...), custom_call_target="tpu_custom_call" | custom-call | tf_op jit(solution)/shard_map/pallas_call | solution.py:508
  134.6 8.9 %shard_map.374.q_grad = bf16[64,2560]{1,0:T(8,128)(2,1)} custom-call(bf16[80,2048]{1,0:T(8,128)(2,1)} %get-tuple-element.48.long_tab, bf16[160,2048]{1,0:T(8,128)(2,1)} %get-tuple-element.49.short_tab, f32[64,2560]{1,0:T(8,128)} %get-tuple-element.57.grad, f32[1,2560]{1,0:T(1,128)} %get-tuple-element.62.denom, f32[1,2560]{1,0:T(1,128)} %get-tuple-element.55.scale, ...), custom_call_target="tpu_custom_call" | custom-call | tf_op jit(solution)/shard_map/pallas_call | solution.py:508
  143.6 14.5 %shard_map.373 = (bf16[80,2048]{1,0:T(8,128)(2,1)}, bf16[64,128]{1,0:T(8,128)(2,1)}, bf16[64,128]{1,0:T(8,128)(2,1)}) custom-call(bf16[80,2048]{1,0:T(8,128)(2,1)} %get-tuple-element.56.part, bf16[64,128]{1,0:T(8,128)(2,1)} %get-tuple-element.179.first, bf16[64,128]{1,0:T(8,128)(2,1)} %get-tuple-element.178.last), custom_call_target="tpu_custom_call" | custom-call | tf_op jit(solution)/shard_map/pallas_call | solution.py:519
  158.1 15.3 %shard_map.375 = (bf16[16,3,80,128]{3,2,1,0:T(8,128)(2,1)}, f32[192,768]{1,0:T(8,128)}, f32[192,1]{1,0:T(8,128)}, f32[1,256]{1,0:T(1,128)}) custom-call(bf16[80,2048]{1,0:T(8,128)(2,1)} %get-tuple-element.58.long_tab, bf16[160,2048]{1,0:T(8,128)(2,1)} %get-tuple-element.59.short_tab, f32[64,2560]{1,0:T(8,128)} %get-tuple-element.57.grad, ...), custom_call_target="tpu_custom_call" | custom-call | tf_op jit(solution)/shard_map/pallas_call | solution.py:508
  175.3 3.7 convolution_convert_fusion.1
  179.0 3.6 convolution_convert_fusion
  184.3 72.3 %all-reduce.6.cloned.1.call-done = bf16[1,192,768]{2,1,0:T(8,128)(2,1)} async-done(((bf16[1,192,768]{2,1,0:T(8,128)(2,1)}), bf16[1,192,768]{2,1,0:T(8,128)(2,1)}) %all-reduce.6.cloned.1.call-update) | async-done | bytes 294928 | tf_op jit(solution)/shard_map/psum | solution.py:708
  256.9 17.5 %psum.43 = f32[1,257]{1,0:T(1,128)S(1)} all-reduce(f32[1,257]{1,0:T(1,128)S(1)} %all_gather.14), channel_id=1, replica_groups=mesh['zh'=2,'x'=4,'c'=2,'y'=4,'zl'=2] {'zh','x'}, use_global_device_ids=true, to_apply=%region_10.11 | all-reduce | flops 257 | bytes 2056 | tf_op jit(solution)/shard_map/psum | solution.py:708
  274.5 38.3 %all-gather = f32[16,1,257]{2,1,0:T(1,128)S(1)} all-gather(f32[1,1,257]{2,1,0:T(1,128)S(1)} %bitcast.110), channel_id=1, replica_groups=mesh['zh'=2,'x'=4,'c'=2,'y'=4,'zl'=2] {'c','y','zl'}, dimensions={0}, use_global_device_ids=true | all-gather | bytes 17476 | tf_op jit(solution)/shard_map/all_gather | solution.py:708
  313.6 62.6 %psum.45 = f32[7680]{0:T(1024)S(1)} all-reduce(f32[7680]{0:T(1024)S(1)} %constant_dynamic-update-slice_fusion), channel_id=1, replica_groups=mesh['zh'=2,'x'=4,'c'=2,'y'=4,'zl'=2] {'zh','x','c','y','zl'}, use_global_device_ids=true, to_apply=%region_19.20 | all-reduce | flops 7680 | bytes 61440 | tf_op jit(solution)/shard_map/psum | solution.py:726
  376.8 19.6 %shard_map.376 = bf16[12,3,80,128]{3,2,1,0:T(8,128)(2,1)} custom-call(bf16[16,3,80,128]{3,2,1,0:T(8,128)(2,1)} %get-tuple-element.63.chunks), custom_call_target="tpu_custom_call" | custom-call | tf_op jit(solution)/shard_map/pallas_call | solution.py:519
  411.6 24.0 %all-reduce.8.cloned.1.call-done = (bf16[768,768]{1,0:T(8,128)(2,1)}, bf16[768,3072]{1,0:T(8,128)(2,1)}, bf16[3072,768]{1,0:T(8,128)(2,1)}) async-done(((bf16[768,768]{1,0:T(8,128)(2,1)}, bf16[768,3072]{1,0:T(8,128)(2,1)}, bf16[3072,768]{1,0:T(8,128)(2,1)}), (bf16[768,768]{1,0:T(8,128)(2,1)}, bf16[768,3072]{1,0:T(8,128)(2,1)}, bf16[3072,768]{1,0:T(8,128)(2,1)})) %all-reduce.8.cloned.1.call-update) | async-done | bytes 10616848 | tf_op jit(solution)/shard_map/psum | solution.py:719
  438.6 7.4 %convert_element_type.81 = f32[768,3072]{1,0:T(8,128)} convert(bf16[768,3072]{1,0:T(8,128)(2,1)} %get-tuple-element.153) | non-fusion elementwise | flops 2359296 | bytes 14155776 | tf_op jit(solution)/shard_map/convert_element_type | solution.py:718
  446.1 4.5 convert_element_type.83
  450.5 24.0 %all-gather.3.cloned.1.call-done = bf16[16,192,768]{2,1,0:T(8,128)(2,1)} async-done(((bf16[1,192,768]{2,1,0:T(8,128)(2,1)}), bf16[16,192,768]{2,1,0:T(8,128)(2,1)}) %all-gather.3.cloned.1.call-update) | async-done | bytes 4718608 | tf_op jit(solution)/shard_map/all_gather | solution.py:708
  480.1 3.0 copy.136
  483.1 3.0 copy.135
  (196 shorter events, 70.0 us)
Async XLA Ops:
  7.2 85.2 %copy-start = (bf16[768,768]{1,0:T(8,128)(2,1)S(1)}, bf16[768,768]{1,0:T(8,128)(2,1)}, u32[]{:S(2)}) copy-start(bf16[768,768]{1,0:T(8,128)(2,1)} %param.35) | copy-start | bytes 3538948
  7.2 11.0 %copy-start.18 = (s32[1,12,1280]{2,0,1:T(1,128)S(1)}, s32[1,12,1280]{2,0,1:T(1,128)}, u32[]{:S(2)}) copy-start(s32[1,12,1280]{2,0,1:T(1,128)} %param.26) | copy-start | bytes 184324
  7.2 11.0 %copy-start.19 = (s32[1,12,1280]{2,0,1:T(1,128)S(1)}, s32[1,12,1280]{2,0,1:T(1,128)}, u32[]{:S(2)}) copy-start(s32[1,12,1280]{2,0,1:T(1,128)} %param.25) | copy-start | bytes 184324
  7.2 249.3 %all-reduce.6.cloned.1.call-start = ((), (), s32[]{:S(2)}) async-start(), calls=%async_computation | async-start | bytes 589824 | tf_op jit(solution)/shard_map/psum | solution.py:708
  12.5 20.3 %copy-start.12 = (f32[8,2816]{1,0:T(8,128)}, f32[8,2816]{1,0:T(8,128)S(1)}, u32[]{:S(2)}) copy-start(f32[8,2816]{1,0:T(8,128)S(1)} %convert_element_type.67.masks) | copy-start | bytes 270340
  72.0 20.4 %copy-start.30 = (f32[768]{0:T(1024)S(1)}, f32[768]{0:T(1024)}, u32[]{:S(2)}) copy-start(f32[768]{0:T(1024)} %param.36) | copy-start | bytes 9220
  92.4 8.9 %slice-start.3 = ((s8[4718592]{0:T(1024)(128)(4,1)}), s8[4194304]{0:T(1024)(128)(4,1)S(1)}, s32[]{:S(2)}) async-start(s8[4718592]{0:T(1024)(128)(4,1)} %bitcast.91), calls=%async_computation.6 | async-start | bytes 8388608
  94.3 7.0 %slice-start.4 = ((s8[4718592]{0:T(1024)(128)(4,1)}), s8[524288]{0:T(1024)(128)(4,1)S(1)}, s32[]{:S(2)}) async-start(s8[4718592]{0:T(1024)(128)(4,1)} %bitcast.91), calls=%async_computation.7 | async-start | bytes 1048576
  94.3 7.0 %copy-start.31 = (f32[768]{0:T(1024)S(1)}, f32[768]{0:T(1024)}, u32[]{:S(2)}) copy-start(f32[768]{0:T(1024)} %param.42) | copy-start | bytes 9220
  158.1 17.2 %copy-start.4 = (bf16[160,3072]{1,0:T(8,128)(2,1)S(1)}, bf16[160,3072]{1,0:T(8,128)(2,1)}, u32[]{:S(2)}) copy-start(bf16[160,3072]{1,0:T(8,128)(2,1)} %copy-done.3) | copy-start | bytes 2949124
  175.2 260.4 %all-reduce.8.cloned.1.call-start = ((), (), s32[]{:S(2)}) async-start(), calls=%async_computation.2 | async-start | bytes 21233664 | tf_op jit(solution)/shard_map/psum | solution.py:719
  184.1 72.5 %copy-start.34 = (f32[1,256]{1,0:T(1,128)S(1)}, f32[1,256]{1,0:T(1,128)}, u32[]{:S(2)}) copy-start(f32[1,256]{1,0:T(1,128)} %get-tuple-element.66) | copy-start | bytes 3076
  184.1 72.6 %copy-start.17 = (f32[192,1]{1,0:T(8,128)S(1)}, f32[192,1]{1,0:T(8,128)}, u32[]{:S(2)}) copy-start(f32[192,1]{1,0:T(8,128)} %get-tuple-element.65) | copy-start | bytes 2308
  184.1 129.3 %copy-start.26 = (f32[768]{0:T(1024)S(1)}, f32[768]{0:T(1024)}, u32[]{:S(2)}) copy-start(f32[768]{0:T(1024)} %get-tuple-element.159) | copy-start | bytes 9220
  184.1 129.3 %copy-start.21 = (f32[768]{0:T(1024)S(1)}, f32[768]{0:T(1024)}, u32[]{:S(2)}) copy-start(f32[768]{0:T(1024)} %get-tuple-element.145) | copy-start | bytes 9220
  184.1 129.3 %copy-start.20 = (f32[768]{0:T(1024)S(1)}, f32[768]{0:T(1024)}, u32[]{:S(2)}) copy-start(f32[768]{0:T(1024)} %get-tuple-element.148) | copy-start | bytes 9220
  184.1 129.3 %copy-start.25 = (f32[768]{0:T(1024)S(1)}, f32[768]{0:T(1024)}, u32[]{:S(2)}) copy-start(f32[768]{0:T(1024)} %get-tuple-element.157) | copy-start | bytes 9220
  184.1 129.4 %copy-start.24 = (f32[768]{0:T(1024)S(1)}, f32[768]{0:T(1024)}, u32[]{:S(2)}) copy-start(f32[768]{0:T(1024)} %get-tuple-element.143) | copy-start | bytes 9220
  184.2 129.4 %copy-start.23 = (f32[768]{0:T(1024)S(1)}, f32[768]{0:T(1024)}, u32[]{:S(2)}) copy-start(f32[768]{0:T(1024)} %get-tuple-element.147) | copy-start | bytes 9220
  184.2 129.4 %copy-start.27 = (f32[3072]{0:T(1024)S(1)}, f32[3072]{0:T(1024)}, u32[]{:S(2)}) copy-start(f32[3072]{0:T(1024)} %get-tuple-element.155) | copy-start | bytes 36868
  184.2 290.3 %all-gather.3.cloned.1.call-start = ((), (), s32[]{:S(2)}) async-start(), calls=%async_computation.1 | async-start | bytes 5013504 | tf_op jit(solution)/shard_map/all_gather | solution.py:708
  403.1 6.6 %copy-start.9 = (bf16[768,768]{1,0:T(8,128)(2,1)S(1)}, bf16[768,768]{1,0:T(8,128)(2,1)}, u32[]{:S(2)}) copy-start(bf16[768,768]{1,0:T(8,128)(2,1)} %param.30) | copy-start | bytes 3538948
  435.6 10.4 %slice-start.1 = ((s8[4718592]{0:T(1024)(128)(4,1)}), s8[4194304]{0:T(1024)(128)(4,1)S(1)}, s32[]{:S(2)}) async-start(s8[4718592]{0:T(1024)(128)(4,1)} %bitcast.89), calls=%async_computation.4 | async-start | bytes 8388608
  438.6 7.4 %slice-start.2 = ((s8[4718592]{0:T(1024)(128)(4,1)}), s8[524288]{0:T(1024)(128)(4,1)S(1)}, s32[]{:S(2)}) async-start(s8[4718592]{0:T(1024)(128)(4,1)} %bitcast.89), calls=%async_computation.5 | async-start | bytes 1048576
  (21 other events, 55.3 us)
Sparse Core Ops, SparseCore 0:
  175.3 81.1 all-reduce.5
  263.6 171.9 all-reduce.7
  437.3 37.1 all-gather.2

commit v2 on v1

--- a/solution.py
+++ b/solution.py
@@ -320,7 +320,11 @@
     for k in range(3):
         rows_ref[...] = jnp.transpose(g_all[k * HEAD : (k + 1) * HEAD, :].astype(F32))
         pack(rows_ref, grad_out, k)
-    w_out[...] = nn(g_all[...], tok[...])
+    w_grad = jnp.transpose(nn(g_all[...], tok[...]))
+    w_out[:D] = w_grad[:, : 2 * HEAD].astype(BF)
+    w_out[D:] = jnp.concatenate(
+        [w_grad[: D // 2, 2 * HEAD :], w_grad[D // 2 :, 2 * HEAD :]], axis=1
+    ).astype(BF)
     b_out[...] = jnp.sum(g_all[...].astype(F32), axis=1, keepdims=True)
 
 
@@ -330,6 +334,18 @@
 
 def block_id(block):
     return {"zh": block // 4, "x": block % 4}
+
+
+def owns(member):
+    return (member < 8) | (member % 2 == ((member % 8) // 2) % 2)
+
+
+def head_at(member):
+    return jnp.where(member < 8, member, 8 + (member % 8) // 2)
+
+
+def owner_of(head):
+    return head if head < 8 else 8 + (head - 8) * 2 + (head - 8) % 2
 
 
 def my_member():
@@ -368,8 +384,7 @@
     def codes_to(d):
         to = (me + d) % MEMBERS
         return to, send(
-            both.at[jnp.minimum(to, HEADS - 1)], codes_out.at[me], send_sem.at[d],
-            recv_sem.at[me], member_id(to),
+            both.at[head_at(to)], codes_out.at[me], send_sem.at[d], recv_sem.at[me], member_id(to)
         )
 
     def planes_to(d):
@@ -378,10 +393,10 @@
 
     for d in range(1, MEMBERS):
         to, copy = codes_to(d)
-        pl.when(to < HEADS)(copy.start)
+        pl.when(owns(to))(copy.start)
     for d in range(1, 8):
         planes_to(d).start()
-    own_codes = pltpu.make_async_copy(both.at[jnp.minimum(me, HEADS - 1)], codes_out.at[me], local.at[1])
+    own_codes = pltpu.make_async_copy(both.at[head_at(me)], codes_out.at[me], local.at[1])
     own_codes.start()
     own_planes = pltpu.make_async_copy(planes, planes_out.at[mine], local.at[2])
     own_planes.start()
@@ -390,10 +405,10 @@
     own_planes.wait()
     for d in range(1, MEMBERS):
         to, copy = codes_to(d)
-        pl.when(to < HEADS)(copy.wait_send)
+        pl.when(owns(to))(copy.wait_send)
         came = (me + d) % MEMBERS
         got = send(both.at[0], codes_out.at[came], send_sem.at[d], recv_sem.at[came], member_id(came))
-        pl.when(me < HEADS)(got.wait_recv)
+        pl.when(owns(me))(got.wait_recv)
     for d in range(1, 8):
         planes_to(d).wait_send()
         came = (mine + d) % 8
@@ -409,8 +424,8 @@
 def scatter_kernel(chunks, out, local, send_sem, recv_sem):
     me = my_member()
     greet([member_id((me + d) % MEMBERS) for d in range(1, MEMBERS)])
-    owner = me < HEADS
-    mine = jnp.minimum(me, HEADS - 1)
+    owner = owns(me)
+    mine = head_at(me)
 
     def to(d):
         dest = (me + d) % MEMBERS
@@ -421,8 +436,9 @@
     keep = pltpu.make_async_copy(chunks.at[me], out.at[mine], local)
     pl.when(owner)(keep.start)
     for h in range(HEADS):
-        got = send(chunks.at[0], out.at[h], send_sem.at[0], recv_sem.at[h], member_id(h))
-        pl.when(me != h)(got.wait_recv)
+        at = owner_of(h)
+        got = send(chunks.at[0], out.at[h], send_sem.at[0], recv_sem.at[h], member_id(at))
+        pl.when(me != at)(got.wait_recv)
     for d in range(1, MEMBERS):
         pl.when(owner)(to(d).wait_send)
     pl.when(owner)(keep.wait)
@@ -431,16 +447,15 @@
 def gather_kernel(chunks, out, local, send_sem, recv_sem):
     me = my_member()
     greet([member_id((me + d) % MEMBERS) for d in range(1, MEMBERS)])
-    owner = me < HEADS
-    mine = jnp.minimum(me, HEADS - 1)
+    owner = owns(me)
+    mine = head_at(me)
 
     def to(d):
         dest = (me + d) % MEMBERS
         copy = send(
-            chunks.at[jnp.minimum(dest, HEADS - 1)], out.at[me], send_sem.at[d], recv_sem.at[me],
-            member_id(dest),
+            chunks.at[head_at(dest)], out.at[me], send_sem.at[d], recv_sem.at[me], member_id(dest)
         )
-        return dest < HEADS, copy
+        return owns(dest), copy
 
     for d in range(1, MEMBERS):
         wanted, copy = to(d)
@@ -504,6 +519,438 @@
     to_up.wait()
 
 
+def norm_forward(values):
+    centred = values - jnp.mean(values, axis=-1, keepdims=True)
+    recip = lax.rsqrt(jnp.mean(centred * centred, axis=-1, keepdims=True) + EPS_NORM)
+    return centred * recip, recip
+
+
+def norm_backward(grad, hat, recip, gain):
+    scaled = grad * gain
+    mean = jnp.mean(scaled, axis=-1, keepdims=True)
+    along = jnp.mean(scaled * hat, axis=-1, keepdims=True)
+    return recip * (scaled - mean - hat * along)
+
+
+def column_sums(values):
+    return jnp.sum(values, axis=0, keepdims=True)
+
+
+def ffn_kernel(
+    att, tok, cot, w_out, w_in, w_back, b_out, ln1_gain, ln1_bias, b_in, b_back, ln2_gain, ln2_bias,
+    output, resid, chunks, big, vec,
+    w_out_v, w_in_v, w_back_v, act_v, slope_v, sems,
+):
+    loads = [
+        pltpu.make_async_copy(a, b, sems.at[k])
+        for k, (a, b) in enumerate([(w_out, w_out_v), (w_in, w_in_v), (w_back, w_back_v)])
+    ]
+    for load in loads:
+        load.start()
+    half = OWN // 2
+    pairs = []
+    for i in range(HEADS // 2):
+        a, b = att[2 * i], att[2 * i + 1]
+        top = jnp.concatenate([a[:, :HEAD], b[:, :HEAD]], axis=1)
+        low = jnp.concatenate([a[:, HEAD:], b[:, HEAD:]], axis=1)
+        pairs.append(jnp.concatenate([top, low], axis=0))
+    attended = jnp.concatenate(pairs, axis=1)
+    loads[0].wait()
+    branch = nn(attended, w_out_v[...]) + b_out[...]
+    hat1, recip1 = norm_forward(tok[...].astype(F32) + branch)
+    hidden = hat1 * ln1_gain[...] + ln1_bias[...]
+    hidden_low = hidden.astype(BF)
+    loads[1].wait()
+    outer = b_back[...]
+    for k in range(FF // D):
+        cols = slice(k * D, (k + 1) * D)
+        inner = nn(hidden_low, w_in_v[:, cols]) + b_in[:, cols]
+        phi = 0.5 * (1.0 + lax.erf(inner * (2.0**-0.5)))
+        slope_v[:, cols] = phi + inner * (jnp.exp(-0.5 * inner * inner) * 0.3989422804014327)
+        act = (inner * phi).astype(BF)
+        act_v[:, cols] = act
+        if k == 0:
+            loads[2].wait()
+        outer = outer + nn(act, w_back_v[cols, :])
+    hat2, recip2 = norm_forward(hidden + outer)
+    output[...] = hat2 * ln2_gain[...] + ln2_bias[...]
+    got = cot[...]
+    sum_grad = norm_backward(got, hat2, recip2, ln2_gain[...])
+    outer_grad = sum_grad.astype(BF)
+    hidden_grad = sum_grad
+    sums = [column_sums(outer_grad.astype(F32)), column_sums(got * hat2), column_sums(got)]
+    hidden_t = jnp.transpose(hidden).astype(BF)
+    bias_rows = []
+    for k in range(FF // D):
+        cols = slice(k * D, (k + 1) * D)
+        act_grad = nt(outer_grad, w_back_v[cols, :])
+        inner_grad = (act_grad * slope_v[:, cols]).astype(BF)
+        bias_rows.append(column_sums(inner_grad.astype(F32)))
+        hidden_grad = hidden_grad + nt(inner_grad, w_in_v[:, cols])
+        into = nn(hidden_t, inner_grad).astype(BF)
+        back = nn(jnp.transpose(act_v[:, cols].astype(F32)).astype(BF), outer_grad).astype(BF)
+        for side in range(2):
+            lanes = slice(side * D // 2, (side + 1) * D // 2)
+            big[2 * k + side] = into[:, lanes]
+            big[8 + 2 * k + side] = back[:, lanes]
+    grad1 = norm_backward(hidden_grad, hat1, recip1, ln1_gain[...])
+    resid[...] = grad1
+    branch_grad = grad1.astype(BF)
+    att_grad = nt(branch_grad, w_out_v[...])
+    for i in range(HEADS // 2):
+        pair = att_grad[:, 2 * i * HEAD : 2 * (i + 1) * HEAD]
+        for side in range(2):
+            lanes = slice(side * HEAD, (side + 1) * HEAD)
+            chunks[2 * i + side] = jnp.concatenate([pair[:half, lanes], pair[half:, lanes]], axis=1).astype(BF)
+    into = nn(jnp.transpose(attended.astype(F32)).astype(BF), branch_grad).astype(BF)
+    for side in range(2):
+        big[16 + side] = into[:, side * D // 2 : (side + 1) * D // 2]
+    rows = [column_sums(branch_grad.astype(F32)), column_sums(hidden_grad * hat1), column_sums(hidden_grad)]
+    vec[...] = jnp.concatenate(rows + sums + bias_rows + [jnp.zeros((6, D), F32)], axis=0)
+
+
+AXES = ("c", "x", "y", "z")
+ORDERS = (("x", "y", "z"), ("y", "z", "x"), ("z", "x", "y"))
+PARTS = 3
+HALF_ROWS = 6912
+PART_ROWS = HALF_ROWS // PARTS
+QUARTER = PART_ROWS // 4
+SIXTEENTH = QUARTER // 4
+SHARE = 144
+CUTS = ((0, 80), (80, 64))
+
+
+def on_axis(axis, k):
+    return {"zh": k // 2, "zl": k % 2} if axis == "z" else {axis: k}
+
+
+def here():
+    spot = {a: lax.axis_index(a) for a in ALL_AXES}
+    spot["z"] = spot["zh"] * 2 + spot["zl"]
+    return spot
+
+
+class Slots:
+    def __init__(self, send_sem, recv_sem):
+        self.send_sem, self.recv_sem, self.used = send_sem, recv_sem, 0
+
+    def take(self):
+        k = self.used
+        self.used += 1
+        return self.send_sem.at[k], self.recv_sem.at[k]
+
+
+class VectorSum:
+    def __init__(self, spot, slots, value, buffer):
+        self.spot, self.value, self.buffer, self.copies = spot, value, buffer, {}
+        for stage, axis in enumerate(AXES):
+            size = 2 if axis == "c" else 4
+            self.copies[stage] = []
+            for d in range(1, size):
+                k = spot[axis]
+                here_ref = buffer.at[stage, k]
+                copy = send(here_ref, here_ref, *slots.take(), on_axis(axis, (k + d) % size))
+                self.copies[stage].append(copy)
+
+    def start(self, stage):
+        self.buffer[stage, self.spot[AXES[stage]]] = self.value
+        for copy in self.copies[stage]:
+            copy.start()
+
+    def finish(self, stage):
+        for copy in self.copies[stage]:
+            copy.wait()
+        total = self.buffer[stage, 0] + self.buffer[stage, 1]
+        if stage > 0:
+            total = total + (self.buffer[stage, 2] + self.buffer[stage, 3])
+        self.value = total
+
+
+def add_rows(count, step, body):
+    def one(i, _):
+        body(pl.multiple_of(i * step, 16))
+        return 0
+
+    lax.fori_loop(0, count // step, one, 0)
+
+
+class BigSum:
+    def __init__(self, spot, slots, source, half, first, first_sum, second, third, result):
+        self.spot, self.source, self.half, self.result = spot, source, half, result
+        self.first, self.first_sum, self.second, self.third = first, first_sum, second, third
+        c = spot["c"]
+        self.copies = {}
+        for a in range(PARTS):
+            one, two, three = ORDERS[a]
+            i, j, k = spot[one], spot[two], spot[three]
+            away = self.rows((1 - c) * HALF_ROWS + a * PART_ROWS, PART_ROWS)
+            inside = pl.ds(a * PART_ROWS, PART_ROWS)
+            sibling = on_axis("c", 1 - c)
+            self.copies[0, a] = [send(source.at[away], half.at[inside], *slots.take(), sibling)]
+            self.copies[1, a] = []
+            self.copies[2, a] = []
+            self.copies[3, a] = []
+            self.copies[4, a] = []
+            self.copies[5, a] = []
+            at = c * HALF_ROWS + a * PART_ROWS
+            quarter = self.rows(at + i * QUARTER, QUARTER)
+            own = self.rows(at + i * QUARTER + j * SIXTEENTH, SIXTEENTH)
+            for d in range(1, 4):
+                to = (i + d) % 4
+                piece = half.at[self.rows(a * PART_ROWS + to * QUARTER, QUARTER)]
+                self.copies[1, a].append(send(piece, first.at[a, d - 1], *slots.take(), on_axis(one, to)))
+                to = (j + d) % 4
+                piece = first_sum.at[a, self.rows(to * SIXTEENTH, SIXTEENTH)]
+                self.copies[2, a].append(send(piece, second.at[a, d - 1], *slots.take(), on_axis(two, to)))
+                to = (k + d) % 4
+                piece = third.at[a, k]
+                self.copies[3, a].append(send(piece, piece, *slots.take(), on_axis(three, to)))
+                to = (j + d) % 4
+                self.copies[4, a].append(send(result.at[own], result.at[own], *slots.take(), on_axis(two, to)))
+                to = (i + d) % 4
+                self.copies[5, a].append(
+                    send(result.at[quarter], result.at[quarter], *slots.take(), on_axis(one, to))
+                )
+            whole = self.rows(at, PART_ROWS)
+            self.copies[6, a] = [send(result.at[whole], result.at[whole], *slots.take(), sibling)]
+
+    @staticmethod
+    def rows(start, count):
+        return pl.ds(pl.multiple_of(start, 16), count)
+
+    def start(self, stage, a):
+        for copy in self.copies[stage, a]:
+            copy.start()
+
+    def finish(self, stage, a):
+        for copy in self.copies[stage, a]:
+            copy.wait()
+        spot = self.spot
+        one, two, three = ORDERS[a]
+        i, j, k = spot[one], spot[two], spot[three]
+        at = spot["c"] * HALF_ROWS + a * PART_ROWS
+        if stage == 0:
+
+            def body(r):
+                got = self.half[self.rows(a * PART_ROWS + r, 128)].astype(F32)
+                mine = self.source[self.rows(at + r, 128)].astype(F32)
+                self.half[self.rows(a * PART_ROWS + r, 128)] = (got + mine).astype(BF)
+
+            add_rows(PART_ROWS, 128, body)
+        if stage == 1:
+
+            def body(r):
+                total = self.half[self.rows(a * PART_ROWS + i * QUARTER + r, 96)].astype(F32)
+                for d in range(3):
+                    total = total + self.first[a, d, self.rows(r, 96)].astype(F32)
+                self.first_sum[a, self.rows(r, 96)] = total.astype(BF)
+
+            add_rows(QUARTER, 96, body)
+        if stage == 2:
+            total = self.first_sum[a, self.rows(j * SIXTEENTH, SIXTEENTH)].astype(F32)
+            for d in range(3):
+                total = total + self.second[a, d].astype(F32)
+            self.third[a, k] = total.astype(BF)
+        if stage == 3:
+            low = self.third[a, 0].astype(F32) + self.third[a, 1].astype(F32)
+            high = self.third[a, 2].astype(F32) + self.third[a, 3].astype(F32)
+            own = self.rows(at + i * QUARTER + j * SIXTEENTH, SIXTEENTH)
+            self.result[own] = (low + high).astype(BF)
+
+
+class HeadSum:
+    def __init__(self, spot, slots, source, got, even, odd):
+        self.spot, self.source, self.got, self.even, self.odd = spot, source, got, even, odd
+        c, x, y, zh, zl, z = (spot[a] for a in ("c", "x", "y", "zh", "zl", "z"))
+        self.block = zh * 4 + x
+        self.is_even, self.is_odd = c == 0, c == 1
+        self.active = (c == 0) | (zl == y % 2)
+        self.pieces = []
+        for d in range(1, BLOCKS):
+            to = (self.block + d) % BLOCKS
+            piece = source.at[pl.ds(pl.multiple_of(to * SHARE, 16), SHARE)]
+            self.pieces.append(send(piece, got.at[d - 1], *slots.take(), block_id(to)))
+        self.copies = {}
+        for side, (ref, count) in enumerate(((even, 0), (odd, 1))):
+            def region(zh_, zl_, x_, y_, lo, n, ref=ref, side=side):
+                spots = (zh_, zl_, x_, y_) if side == 0 else (zh_, x_, y_)
+                return ref.at[(*spots, pl.ds(lo, n))]
+
+            all2, all4 = slice(None), slice(None)
+            self.copies[0, side] = [
+                send(region(zh, zl, x, y, 0, SHARE), region(zh, zl, x, y, 0, SHARE), *slots.take(),
+                     on_axis("z", (z + d) % 4))
+                for d in range(1, 4)
+            ]
+            for part, (lo, n) in enumerate(CUTS):
+                axes = ("x", "y") if part == 0 else ("y", "x")
+                two = region(all2, all2, x, y, lo, n)
+                if axes[1] == "y":
+                    three = region(all2, all2, all4, y, lo, n)
+                else:
+                    three = region(all2, all2, x, all4, lo, n)
+                for stage, piece in ((1, two), (2, three)):
+                    axis = axes[stage - 1]
+                    self.copies[stage, side, part] = [
+                        send(piece, piece, *slots.take(), on_axis(axis, (spot[axis] + d) % 4))
+                        for d in range(1, 4)
+                    ]
+                whole = region(all2, all2, all4, all4, lo, n)
+                self.copies[3, side, part] = [send(whole, whole, *slots.take(), on_axis("c", 1 - c))]
+
+    def start_sum(self):
+        for copy in self.pieces:
+            pl.when(self.active)(copy.start)
+
+    def finish_sum(self):
+        spot = self.spot
+
+        def body():
+            for copy in self.pieces:
+                copy.wait()
+            total = self.source[pl.ds(pl.multiple_of(self.block * SHARE, 16), SHARE)].astype(F32)
+            for d in range(BLOCKS - 1):
+                total = total + self.got[d].astype(F32)
+            total = total.astype(BF)
+
+            def keep_even():
+                self.even[spot["zh"], spot["zl"], spot["x"], spot["y"]] = total
+
+            def keep_odd():
+                self.odd[spot["zh"], spot["x"], spot["y"]] = total
+
+            pl.when(self.is_even)(keep_even)
+            pl.when(self.is_odd)(keep_odd)
+
+        pl.when(self.active)(body)
+
+    def start_z(self):
+        def even():
+            for copy in self.copies[0, 0]:
+                copy.start()
+
+        def odd():
+            for copy in self.copies[0, 1]:
+                copy.start()
+
+        pl.when(self.is_even)(even)
+        pl.when(self.is_odd & self.active)(odd)
+
+    def finish_z(self):
+        def even():
+            for copy in self.copies[0, 0]:
+                copy.wait()
+
+        def odd_send():
+            for copy in self.copies[0, 1]:
+                copy.wait_send()
+
+        pl.when(self.is_even)(even)
+        pl.when(self.is_odd & self.active)(odd_send)
+        for d in range(1, 4):
+            came = (self.spot["z"] + 4 - d) % 4
+            sent = self.is_odd & (came % 2 == self.spot["y"] % 2)
+            pl.when(sent)(self.copies[0, 1][d - 1].wait_recv)
+
+    def start(self, stage, part):
+        for side, mine in enumerate((self.is_even, self.is_odd)):
+
+            def go(side=side):
+                for copy in self.copies[stage, side, part]:
+                    copy.start()
+
+            pl.when(mine)(go)
+
+    def finish(self, stage, part):
+        for side, mine in enumerate((self.is_even, self.is_odd)):
+
+            def go(side=side):
+                for copy in self.copies[stage, side, part]:
+                    copy.wait()
+
+            pl.when(mine)(go)
+
+    def start_core(self, part):
+        for side, mine in enumerate((self.is_even, self.is_odd)):
+            pl.when(mine)(self.copies[3, side, part][0].start)
+
+    def finish_core(self, part):
+        for side, mine in enumerate((self.is_even, self.is_odd)):
+            pl.when(mine)(self.copies[3, side, part][0].wait_send)
+            pl.when(~mine)(self.copies[3, side, part][0].wait_recv)
+
+
+def sum_peers(spot):
+    ids = [on_axis("c", 1 - spot["c"])]
+    for axis in ("x", "y", "z"):
+        ids += [on_axis(axis, (spot[axis] + d) % 4) for d in range(1, 4)]
+    ids += [{"zh": 1 - spot["zh"], "x": (spot["x"] + d) % 4} for d in range(1, 4)]
+    return ids
+
+
+BIG_SLOTS = PARTS * (1 + 5 * 3 + 1)
+HEAD_SLOTS = 7 + 2 * (3 + 2 * (3 + 3 + 1))
+VEC_SLOTS = 1 + 3 * 3
+
+
+def weight_kernel(
+    big, vec, head_w, big_out, vec_out, even, odd,
+    half, first, first_sum, second, third, got, vec_buf, send_sem, recv_sem,
+):
+    spot = here()
+    greet(sum_peers(spot))
+    slots = Slots(send_sem, recv_sem)
+    sums = BigSum(spot, slots, big, half, first, first_sum, second, third, big_out)
+    heads = HeadSum(spot, slots, head_w, got, even, odd)
+    vector = VectorSum(spot, slots, vec[...], vec_buf)
+    parts = range(PARTS)
+    for a in parts:
+        sums.start(0, a)
+    heads.start_sum()
+    vector.start(0)
+    for a in parts:
+        sums.finish(0, a)
+        sums.start(1, a)
+    vector.finish(0)
+    vector.start(1)
+    heads.finish_sum()
+    heads.start_z()
+    for a in parts:
+        sums.finish(1, a)
+        sums.start(2, a)
+    vector.finish(1)
+    vector.start(2)
+    heads.finish_z()
+    for part in range(2):
+        heads.start(1, part)
+    for a in parts:
+        sums.finish(2, a)
+        sums.start(3, a)
+    vector.finish(2)
+    vector.start(3)
+    for a in parts:
+        sums.finish(3, a)
+        sums.start(4, a)
+    vector.finish(3)
+    vec_out[...] = vector.value
+    for part in range(2):
+        heads.finish(1, part)
+        heads.start(2, part)
+    for a in parts:
+        sums.finish(4, a)
+        sums.start(5, a)
+    for part in range(2):
+        heads.finish(2, part)
+        heads.start_core(part)
+    for a in parts:
+        sums.finish(5, a)
+        sums.start(6, a)
+    for part in range(2):
+        heads.finish_core(part)
+    for a in parts:
+        sums.finish(6, a)
+
+
 def call(kernel, outs, scratch, *args):
     return pl.pallas_call(
         kernel,
@@ -528,6 +975,19 @@
     )(*args)
 
 
+def local_call(kernel, outs, scratch, far, *args):
+    return pl.pallas_call(
+        kernel,
+        out_shape=[jax.ShapeDtypeStruct(shape, kind) for shape, kind in outs],
+        in_specs=[
+            pl.BlockSpec(memory_space=pl.ANY if k in far else pltpu.VMEM) for k in range(len(args))
+        ],
+        out_specs=[pl.BlockSpec(memory_space=pltpu.VMEM)] * len(outs),
+        scratch_shapes=scratch,
+        compiler_params=pltpu.CompilerParams(vmem_limit_bytes=VMEM_LIMIT),
+    )(*args)
+
+
 def dma(count):
     return pltpu.SemaphoreType.DMA((count,))
 
@@ -551,27 +1011,6 @@
         [pltpu.VMEM((BLOCKS, ITEM, SLOTS), BF), dma(2 * BLOCKS), dma(2 * BLOCKS), dma(2), dma(2)],
         part, first, last,
     )
-
-
-def layer_norm(values, norm_gain, norm_bias):
-    row_mean = jnp.mean(values, axis=-1, keepdims=True)
-    centred = values - row_mean
-    spread = jnp.mean(centred * centred, axis=-1, keepdims=True)
-    return centred * lax.rsqrt(spread + EPS_NORM) * norm_gain + norm_bias
-
-
-def gelu_exact(values):
-    return jax.nn.gelu(values, approximate=False)
-
-
-def to_members(array):
-    return lax.all_to_all(array, MEMBER_AXES, 0, 0, tiled=True)
-
-
-def from_neighbours(first, last):
-    up = [(i, (i + 1) % 8) for i in range(8)]
-    down = [(j, i) for i, j in up]
-    return lax.ppermute(last, BLOCK_AXES, up), lax.ppermute(first, BLOCK_AXES, down)
 
 
 def item_masks(cuts, block):
@@ -598,7 +1037,7 @@
     block = lax.axis_index(BLOCK_AXES)
     member = lax.axis_index(MEMBER_AXES)
     hash_at = lax.axis_index(("y", "zl"))
-    head = jnp.minimum(member, HEADS - 1)
+    head = head_at(member)
     both = jnp.concatenate([q_codes, k_codes], axis=0).transpose(1, 0, 2)
     tok, both, planes = talk(
         start_kernel, 0,
@@ -649,34 +1088,22 @@
         long_tab, short_tab, codes, weights, masks, value, v_before, v_after, v_bias, taps_fwd,
     )
     att = all_to_members(att_rows, 2)
-    attended_low = att.reshape(HEADS, OWN // 2, 2, HEAD).transpose(2, 1, 0, 3).reshape(OWN, D)
-
     own_tokens = lax.dynamic_slice_in_dim(tokens, hash_at * OWN, OWN, 0)
-    branch = nn(attended_low, w_out) + b_out
-    hidden, norm_one_back = jax.vjp(layer_norm, own_tokens.astype(F32) + branch, ln1_gain, ln1_bias)
-    hidden_low = hidden.astype(BF)
-    inner_pre = nn(hidden_low, w_in) + b_in
-    activated, gelu_back = jax.vjp(gelu_exact, inner_pre)
-    activated_low = activated.astype(BF)
-    outer_out = nn(activated_low, w_back) + b_back
-    output, norm_two_back = jax.vjp(layer_norm, hidden + outer_out, ln2_gain, ln2_bias)
-    sum_grad, grad_ln2_gain, grad_ln2_bias = norm_two_back(cotangent)
-    outer_grad = sum_grad.astype(BF)
-    grad_w_back = tn(activated_low, outer_grad)
-    grad_b_back = jnp.sum(outer_grad.astype(F32), axis=0)
-    (inner_grad,) = gelu_back(nt(outer_grad, w_back))
-    inner_low = inner_grad.astype(BF)
-    grad_w_in = tn(hidden_low, inner_low)
-    grad_b_in = jnp.sum(inner_low.astype(F32), axis=0)
-    hidden_grad = sum_grad + nt(inner_low, w_in)
-    resid_grad, grad_ln1_gain, grad_ln1_bias = norm_one_back(hidden_grad)
-    branch_grad = resid_grad.astype(BF)
-    grad_w_out = tn(attended_low, branch_grad)
-    grad_b_out = jnp.sum(branch_grad.astype(F32), axis=0)
-    attended_grad = nt(branch_grad, w_out).astype(BF)
-
-    grad_chunks = attended_grad.reshape(2, OWN // 2, HEADS, HEAD).transpose(2, 1, 0, 3)
-    grad_rows = all_to_owners(grad_chunks.reshape(HEADS, OWN // 2, 2 * HEAD), 3)
+    output, resid_grad, grad_chunks, big, vec = local_call(
+        ffn_kernel,
+        [
+            ((OWN, D), F32), ((OWN, D), F32), ((HEADS, OWN // 2, 2 * HEAD), BF), ((18, D, D // 2), BF),
+            ((16, D), F32),
+        ],
+        [
+            pltpu.VMEM((D, D), BF), pltpu.VMEM((D, FF), BF), pltpu.VMEM((FF, D), BF), pltpu.VMEM((OWN, FF), BF),
+            pltpu.VMEM((OWN, FF), F32), dma(3),
+        ],
+        (3, 4, 5),
+        att, own_tokens, cotangent, w_out, w_in, w_back, b_out[None], ln1_gain[None], ln1_bias[None],
+        b_in[None], b_back[None], ln2_gain[None], ln2_bias[None],
+    )
+    grad_rows = all_to_owners(grad_chunks, 3)
     long_gpart, short_gtab, grad_t, denom = call(
         read_back_kernel,
         [long_shape, short_shape, ((HEAD, BLOCK), F32), ((1, BLOCK), F32)],
@@ -694,7 +1121,7 @@
     )
     grad_qkv, head_w, head_b, head_taps = call(
         key_back_kernel,
-        [((MEMBERS, 3, OWN // 2, 2 * HEAD), BF), ((3 * HEAD, D), F32), ((3 * HEAD, 1), F32), ((1, 256), F32)],
+        [((MEMBERS, 3, OWN // 2, 2 * HEAD), BF), ((D + D // 2, 2 * HEAD), BF), ((3 * HEAD, 1), F32), ((1, 256), F32)],
         [table, ext, ext, ((3 * HEAD, BLOCK), BF), rows_f32],
         long_gtab, short_gtab, grad_t, g_before, g_after, codes, weights, masks, qkv,
         v_before, v_after, planes, v_bias, taps_bwd, q_grad, tok,
@@ -704,29 +1131,47 @@
     lows = lows.reshape(HEADS, 3, OWN // 2, 2, HEAD).transpose(1, 3, 2, 0, 4).reshape(3, OWN, D)
     grad_tokens = resid_grad + nt(lows[0], w_query) + nt(lows[1], w_key) + nt(lows[2], w_value)
 
-    def all_heads(array):
-        return lax.all_gather(lax.psum(array, BLOCK_AXES), MEMBER_AXES, axis=0)[:HEADS]
-
-    heads_w = all_heads(head_w.astype(BF)).astype(F32).reshape(HEADS, 3, HEAD, D)
-    heads_w = heads_w.transpose(1, 3, 0, 2).reshape(3, D, D)
     small = jnp.concatenate([head_b[:, 0], head_taps[0, 96:161][::-1]])
-    heads_small = all_heads(small)
+    small = jnp.pad(small, (0, D // 2 - small.shape[0]))
+    row = lax.broadcasted_iota(jnp.int32, (16, D // 2), 0)
+    small = jnp.where((row == head) & owns(member), small[None], 0.0)
+    wide = D + D // 2
+    big_sum, vec_sum, even, odd = talk(
+        weight_kernel, 5,
+        [
+            ((18 * D, D // 2), BF), ((16, wide), F32), ((2, 2, 4, 4, SHARE, 128), BF),
+            ((2, 4, 4, SHARE, 128), BF),
+        ],
+        [
+            pltpu.VMEM((HALF_ROWS, D // 2), BF), pltpu.VMEM((PARTS, 3, QUARTER, D // 2), BF),
+            pltpu.VMEM((PARTS, QUARTER, D // 2), BF), pltpu.VMEM((PARTS, 3, SIXTEENTH, D // 2), BF),
+            pltpu.VMEM((PARTS, 4, SIXTEENTH, D // 2), BF), pltpu.VMEM((BLOCKS - 1, SHARE, 128), BF),
+            pltpu.VMEM((4, 4, 16, wide), F32), dma(BIG_SLOTS + HEAD_SLOTS + VEC_SLOTS),
+            dma(BIG_SLOTS + HEAD_SLOTS + VEC_SLOTS),
+        ],
+        big.reshape(18 * D, D // 2), jnp.concatenate([vec, small], axis=1), head_w,
+    )
+    by_head = jnp.concatenate(
+        [
+            even.transpose(3, 1, 0, 2, 4, 5).reshape(8, D + D // 2, 2 * HEAD),
+            odd.transpose(2, 0, 1, 3, 4).reshape(4, D + D // 2, 2 * HEAD),
+        ]
+    )
+    two = by_head[:, :D].reshape(HEADS, D, 2, HEAD).transpose(2, 1, 0, 3).reshape(2, D, D)
+    last = by_head[:, D:].reshape(HEADS, D // 2, 2, HEAD).transpose(2, 1, 0, 3).reshape(D, D)
+    heads_w = (two[0].astype(F32), two[1].astype(F32), last.astype(F32))
+    heads_small = vec_sum[:HEADS, D:]
     heads_b = heads_small[:, : 3 * HEAD].reshape(HEADS, 3, HEAD).transpose(1, 0, 2).reshape(3, D)
-    grad_conv_weight = heads_small[:, 3 * HEAD :]
-
-    grad_w_in, grad_w_back, grad_w_out = [
-        part.astype(F32)
-        for part in lax.psum(
-            (grad_w_in.astype(BF), grad_w_back.astype(BF), grad_w_out.astype(BF)), ALL_AXES
-        )
-    ]
-    vectors = (
-        grad_b_out, grad_ln1_gain, grad_ln1_bias, grad_b_back, grad_ln2_gain, grad_ln2_bias, grad_b_in,
-    )
-    joined = lax.psum(jnp.concatenate(vectors), ALL_AXES)
-    (
-        grad_b_out, grad_ln1_gain, grad_ln1_bias, grad_b_back, grad_ln2_gain, grad_ln2_bias, grad_b_in,
-    ) = jnp.split(joined, [D * (k + 1) for k in range(6)])
+    grad_conv_weight = heads_small[:, 3 * HEAD : 3 * HEAD + 65]
+    big_sum = big_sum.reshape(18, D, D // 2)
+    grad_w_in = big_sum[:8].transpose(1, 0, 2).reshape(D, FF).astype(F32)
+    grad_w_back = big_sum[8:16].reshape(4, 2, D, D // 2).transpose(0, 2, 1, 3).reshape(FF, D).astype(F32)
+    grad_w_out = big_sum[16:].transpose(1, 0, 2).reshape(D, D).astype(F32)
+    vectors = vec_sum[:, :D]
+    grad_b_out, grad_ln1_gain, grad_ln1_bias, grad_b_back, grad_ln2_gain, grad_ln2_bias = (
+        vectors[k] for k in range(6)
+    )
+    grad_b_in = vectors[6:10].reshape(FF)
     return (
         output, grad_tokens, heads_w[0], heads_b[0], heads_w[1], heads_b[1], heads_w[2], heads_b[2],
         grad_conv_weight, grad_w_out, grad_b_out, grad_ln1_gain, grad_ln1_bias, grad_w_in, grad_b_in,

time: 496 us -> 411 us (0.83)
  Pallas kernels: 138 us -> 261 us
  waiting for transfers between devices: 120 us -> 0 us
  blocking collectives: 118 us -> 0 us
  local copies, waits for them, and re-layouts: 46.8 us -> 123 us
  matrix products: 28.2 us -> 3.6 us
  between operations: 15.9 us -> 2.9 us
  other arithmetic: 27.1 us -> 14.5 us
    pallas_call x6 -> x7, Pallas kernels: 87.7 us -> 194 us  [talk(): pl.pallas_call(kernel, out_shape=[jax.ShapeDtypeStruct(shape, kind) for s...]
    psum x2 -> x0, waiting for transfers between devices: 96.3 us -> none  [the longest x1 72.3 us: all_heads(): lax.psum(array, BLOCK_AXES)]
    psum x2 -> x0, blocking collectives: 80.1 us -> none  [the longest x1 62.6 us: per_device(): joined = lax.psum(jnp.concatenate(vectors), ALL_AXES)]
    convert_element_type x1 -> x5, local copies, waits for them, and re-layouts: 1.11 us -> 51.5 us  [the longest x1 38.3 us: per_device(): big_sum[8:16].reshape(4, 2, D, D // 2).transpose(0, 2, 1, 3).reshape(FF, D)]
    all_gather x1 -> x0, blocking collectives: 38.3 us -> none  [all_heads(): lax.all_gather(lax.psum(array, BLOCK_AXES), MEMBER_AXES, axis=0)[:HEADS]]
    all_gather x1 -> x0, waiting for transfers between devices: 24 us -> none  [all_heads(): lax.all_gather(lax.psum(array, BLOCK_AXES), MEMBER_AXES, axis=0)[:HEADS]]
    dot_general x6 -> x0, matrix products: 18.5 us -> none  [the longest x3 9.64 us: nn(): lax.dot_general(left, right, (((1,), (0,)), ((), ())), preferred_element_...]
    pallas_call x0 -> x1, Pallas kernels: none -> 17.7 us  [local_call(): pl.pallas_call(kernel, out_shape=[jax.ShapeDtypeStruct(shape, kind) for s...]
  transfers between devices with their start and end apart: 3 -> 0, of which waited for: 3 -> 0; matrix products, arithmetic and copies ran while one was open for 8% -> 0% of each run, Pallas kernels for 4% -> 0%
where the time goes in v2:
time: 411 us; the launch traced here: 405 us
  Pallas kernels  261 us (64%)
  local copies, waits for them, and re-layouts  123 us (30%)
  other arithmetic  14.5 us (4%)
    pallas_call x7, Pallas kernels, talk(): pl.pallas_call(kernel, out_shape=[jax.ShapeDtypeStruct(shape, kind) for s...  194 us
    pallas_call x5, Pallas kernels, call(): pl.pallas_call(kernel, out_shape=[jax.ShapeDtypeStruct(shape, kind) for s...  49.9 us
    convert_element_type x1, local copies, waits for them, and re-layouts, per_device(): big_sum[8:16].reshape(4, 2, D, D // 2).transpose(0, 2, 1, 3).reshape(FF, D)  38.3 us
    pallas_call x1, Pallas kernels, local_call(): pl.pallas_call(kernel, out_shape=[jax.ShapeDtypeStruct(shape, kind) for s...  17.7 us
    unnamed x32, local copies, waits for them, and re-layouts  13.3 us
    slice x1, local copies, waits for them, and re-layouts, per_device(): big_sum[8:16].reshape(4, 2, D, D // 2).transpose(0, 2, 1, 3).reshape(FF, D)  8.46 us

profile of v2, /device:TPU:1, one launch (start us, length us, event | category | flops | bytes accessed | tf_op | source)
XLA Modules:
  0.0 405.0 jit_solution(3589263213864712236)
XLA Ops:
  23.7 13.9 %shard_map.366 = (bf16[2560,768]{1,0:T(8,128)(2,1)}, s32[16,2,1280]{2,1,0:T(2,128)}, f32[8,8,64]{2,1,0:T(8,128)}) custom-call(bf16[1280,768]{1,0:T(8,128)(2,1)} %tokens.1, s32[12,2,1280]{2,1,0:T(2,128)} %add_bitcast_fusion.both, f32[8,64]{1,0:T(8,128)} %bitcast.120), custom_call_target="tpu_custom_call" | custom-call | tf_op jit(solution)/shard_map/pallas_call | solution.py:966
  40.5 11.2 %shard_map.367 = (f32[192,2560]{1,0:T(8,128)}, f32[16,2560]{1,0:T(8,128)}, bf16[80,2048]{1,0:T(8,128)(2,1)}, bf16[160,2048]{1,0:T(8,128)(2,1)}) custom-call(bf16[2560,768]{1,0:T(8,128)(2,1)} %get-tuple-element.52.tok, bf16[192,768]{1,0:T(8,128)(2,1)} %pad_maximum_fusion.1.w_t, f32[192,1]{1,0:T(8,128)} %copy.106.bias, f32[64,64]{1,0:T(8,128)} %bitcast.110, ...), custom_call_target="tpu_custom_call" | custom-call | tf_op jit(solution)/shard_map/pallas_call | solution.py:955
  54.1 18.8 %shard_map.368 = (bf16[80,2048]{1,0:T(8,128)(2,1)}, bf16[64,128]{1,0:T(8,128)(2,1)}, bf16[64,128]{1,0:T(8,128)(2,1)}) custom-call(bf16[80,2048]{1,0:T(8,128)(2,1)} %get-tuple-element.55.part, bf16[64,128]{1,0:T(8,128)(2,1)} %get-tuple-element.161.first, bf16[64,128]{1,0:T(8,128)(2,1)} %get-tuple-element.160.last), custom_call_target="tpu_custom_call" | custom-call | tf_op jit(solution)/shard_map/pallas_call | solution.py:966
  74.1 7.9 %shard_map.369 = (bf16[16,80,128]{2,1,0:T(8,128)(2,1)}, f32[64,2560]{1,0:T(8,128)}, f32[1,2560]{1,0:T(1,128)}) custom-call(bf16[80,2048]{1,0:T(8,128)(2,1)} %get-tuple-element.57.long_tab, bf16[160,2048]{1,0:T(8,128)(2,1)} %get-tuple-element.58.short_tab, s32[2,8,2560]{2,1,0:T(8,128)} %bitcast.101, f32[16,2560]{1,0:T(8,128)} %get-tuple-element.59.weights, ...), custom_call_target="tpu_custom_call" | custom-call | tf_op jit(solution)/shard_map/pallas_call | solution.py:955
  82.0 11.6 %shard_map.370.att = bf16[12,80,128]{2,1,0:T(8,128)(2,1)} custom-call(bf16[16,80,128]{2,1,0:T(8,128)(2,1)} %get-tuple-element.62.chunks), custom_call_target="tpu_custom_call" | custom-call | tf_op jit(solution)/shard_map/pallas_call | solution.py:966
  93.7 17.7 %shard_map.371 = (f32[160,768]{1,0:T(8,128)}, f32[160,768]{1,0:T(8,128)}, bf16[12,80,128]{2,1,0:T(8,128)(2,1)}, bf16[18,768,384]{2,1,0:T(8,128)(2,1)}, f32[16,768]{1,0:T(8,128)}) custom-call(bf16[12,80,128]{2,1,0:T(8,128)(2,1)} %shard_map.370.att, bf16[160,768]{1,0:T(8,128)(2,1)} %constant_dynamic-slice_fusion.tok, f32[160,768]{1,0:T(8,128)} %cot.1, ...), custom_call_target="tpu_custom_call" | custom-call | tf_op jit(solution)/shard_map/pallas_call | solution.py:979
  111.4 10.7 %shard_map.372.chunks = bf16[16,80,128]{2,1,0:T(8,128)(2,1)} custom-call(bf16[12,80,128]{2,1,0:T(8,128)(2,1)} %get-tuple-element.65.chunks), custom_call_target="tpu_custom_call" | custom-call | tf_op jit(solution)/shard_map/pallas_call | solution.py:966
  122.0 6.7 %shard_map.373 = (bf16[80,2048]{1,0:T(8,128)(2,1)}, bf16[160,2048]{1,0:T(8,128)(2,1)}, f32[64,2560]{1,0:T(8,128)}, f32[1,2560]{1,0:T(1,128)}) custom-call(bf16[16,80,128]{2,1,0:T(8,128)(2,1)} %shard_map.372.chunks, f32[64,2560]{1,0:T(8,128)} %get-tuple-element.66.estimate, f32[1,2560]{1,0:T(1,128)} %get-tuple-element.67.scale, s32[2,8,2560]{2,1,0:T(8,128)} %bitcast.102, ...), custom_call_target="tpu_custom_call" | custom-call | tf_op jit(solution)/shard_map/pallas_call | solution.py:955
  128.7 9.0 %shard_map.375.q_grad = bf16[64,2560]{1,0:T(8,128)(2,1)} custom-call(bf16[80,2048]{1,0:T(8,128)(2,1)} %get-tuple-element.57.long_tab, bf16[160,2048]{1,0:T(8,128)(2,1)} %get-tuple-element.58.short_tab, f32[64,2560]{1,0:T(8,128)} %get-tuple-element.69.grad, f32[1,2560]{1,0:T(1,128)} %get-tuple-element.74.denom, f32[1,2560]{1,0:T(1,128)} %get-tuple-element.67.scale, ...), custom_call_target="tpu_custom_call" | custom-call | tf_op jit(solution)/shard_map/pallas_call | solution.py:955
  138.4 15.5 %shard_map.374 = (bf16[80,2048]{1,0:T(8,128)(2,1)}, bf16[64,128]{1,0:T(8,128)(2,1)}, bf16[64,128]{1,0:T(8,128)(2,1)}) custom-call(bf16[80,2048]{1,0:T(8,128)(2,1)} %get-tuple-element.68.part, bf16[64,128]{1,0:T(8,128)(2,1)} %get-tuple-element.163.first, bf16[64,128]{1,0:T(8,128)(2,1)} %get-tuple-element.162.last), custom_call_target="tpu_custom_call" | custom-call | tf_op jit(solution)/shard_map/pallas_call | solution.py:966
  153.8 15.1 %shard_map.376 = (bf16[16,3,80,128]{3,2,1,0:T(8,128)(2,1)}, bf16[1152,128]{1,0:T(8,128)(2,1)}, f32[192,1]{1,0:T(8,128)}, f32[1,256]{1,0:T(1,128)}) custom-call(bf16[80,2048]{1,0:T(8,128)(2,1)} %get-tuple-element.70.long_tab, bf16[160,2048]{1,0:T(8,128)(2,1)} %get-tuple-element.71.short_tab, f32[64,2560]{1,0:T(8,128)} %get-tuple-element.69.grad, ...), custom_call_target="tpu_custom_call" | custom-call | tf_op jit(solution)/shard_map/pallas_call | solution.py:955
  169.0 19.3 %shard_map.377 = bf16[12,3,80,128]{3,2,1,0:T(8,128)(2,1)} custom-call(bf16[16,3,80,128]{3,2,1,0:T(8,128)(2,1)} %get-tuple-element.75.chunks), custom_call_target="tpu_custom_call" | custom-call | tf_op jit(solution)/shard_map/pallas_call | solution.py:966
  194.2 2.1 copy.111
  203.6 103.9 %shard_map.378 = (bf16[13824,384]{1,0:T(8,128)(2,1)}, f32[16,1152]{1,0:T(8,128)}, bf16[2,2,4,4,144,128]{5,4,3,2,1,0:T(8,128)(2,1)}, bf16[2,4,4,144,128]{4,3,2,1,0:T(8,128)(2,1)}) custom-call(bf16[13824,384]{1,0:T(8,128)(2,1)} %bitcast.91, f32[16,1152]{1,0:T(8,128)} %pad_maximum_fusion.2.vec, bf16[1152,128]{1,0:T(8,128)(2,1)} %get-tuple-element.80.head_w), custom_call_target="tpu_custom_call" | custom-call | tf_op jit(solution)/shard_map/pallas_call | solution.py:966
  307.5 2.0 copy.113
  321.0 8.5 %fusion.2 = (bf16[6144,384]{1,0:T(8,128)(2,1)}, bf16[6144,384]{1,0:T(8,128)(2,1)}) fusion(bf16[13824,384]{1,0:T(8,128)(2,1)} %get-tuple-element.84), kind=kLoop, calls=%fused_computation.49 | loop fusion | bytes 18874368 | tf_op jit(solution)/shard_map/slice | solution.py:1168
  334.5 2.8 copy.115
  337.3 3.0 copy.116
  340.4 3.5 copy.117
  345.4 3.0 copy.123
  353.1 3.1 convert_bitcast_fusion.1
  356.2 5.0 %copy.128 = f32[8,96,8,384]{3,2,0,1:T(8,128)} copy(f32[8,96,8,384]{3,2,1,0:T(8,128)S(1)} %convert_bitcast_fusion.1) | data formatting | bytes 18874368 | tf_op jit(solution)/shard_map/convert_element_type | solution.py:1167
  361.9 38.3 %copy.120 = f32[4,768,2,384]{3,2,1,0:T(2,128)S(1)} copy(f32[4,768,2,384]{3,1,2,0:T(8,128)S(1)} %convert_bitcast_fusion) | data formatting | bytes 18874368 | tf_op jit(solution)/shard_map/convert_element_type | solution.py:1168
  400.2 4.4 %copy.130 = f32[384,8,2,384]{3,1,2,0:T(8,128)} copy(f32[384,8,2,384]{3,2,1,0:T(2,128)S(1)} %bitcast.84) | data formatting | bytes 18874368
  (108 shorter events, 65.0 us)
Async XLA Ops:
  0.7 19.0 %copy-start = (bf16[768,768]{1,0:T(8,128)(2,1)S(1)}, bf16[768,768]{1,0:T(8,128)(2,1)}, u32[]{:S(2)}) copy-start(bf16[768,768]{1,0:T(8,128)(2,1)} %param.28) | copy-start | bytes 3538948
  0.7 20.9 %copy-start.4 = (bf16[768,768]{1,0:T(8,128)(2,1)S(1)}, bf16[768,768]{1,0:T(8,128)(2,1)}, u32[]{:S(2)}) copy-start(bf16[768,768]{1,0:T(8,128)(2,1)} %param.30) | copy-start | bytes 3538948
  16.6 21.0 %copy-start.7 = (f32[8,2816]{1,0:T(8,128)}, f32[8,2816]{1,0:T(8,128)S(1)}, u32[]{:S(2)}) copy-start(f32[8,2816]{1,0:T(8,128)S(1)} %convert_element_type.76.masks) | copy-start | bytes 270340
  51.7 21.2 %copy-start.2 = (f32[192,2560]{1,0:T(8,128)S(1)}, f32[192,2560]{1,0:T(8,128)}, u32[]{:S(2)}) copy-start(f32[192,2560]{1,0:T(8,128)} %get-tuple-element.56.qkv) | copy-start | bytes 5898244
  128.7 9.0 %copy-start.3 = (f32[64,2560]{1,0:T(8,128)S(1)}, f32[64,2560]{1,0:T(8,128)}, u32[]{:S(2)}) copy-start(f32[64,2560]{1,0:T(8,128)} %get-tuple-element.69.grad) | copy-start | bytes 1966084
  153.8 36.5 %copy-start.9 = (f32[16,768]{1,0:T(8,128)S(1)}, f32[16,768]{1,0:T(8,128)}, u32[]{:S(2)}) copy-start(f32[16,768]{1,0:T(8,128)} %get-tuple-element.77) | copy-start | bytes 147460
  193.6 4.0 copy-start.6
  200.0 2.3 copy-start.5
  307.5 2.0 copy-start.8
  353.1 8.2 %slice-start = ((s8[4718592]{0:T(1024)(128)(4,1)}), s8[4194304]{0:T(1024)(128)(4,1)S(1)}, s32[]{:S(2)}) async-start(s8[4718592]{0:T(1024)(128)(4,1)} %bitcast.87), calls=%async_computation | async-start | bytes 8388608
  356.2 5.1 %slice-start.1 = ((s8[4718592]{0:T(1024)(128)(4,1)}), s8[524288]{0:T(1024)(128)(4,1)S(1)}, s32[]{:S(2)}) async-start(s8[4718592]{0:T(1024)(128)(4,1)} %bitcast.87), calls=%async_computation.1 | async-start | bytes 1048576
  400.2 4.4 %copy-start.1 = (bf16[768,768]{1,0:T(8,128)(2,1)S(1)}, bf16[768,768]{1,0:T(8,128)(2,1)}, u32[]{:S(2)}) copy-start(bf16[768,768]{1,0:T(8,128)(2,1)} %param.28) | copy-start | bytes 3538948
